TPU v7x, 1024 devices: a whole 4x4x32 slice. The times are simulated.
1024 devices in a mesh: dp: 128 (over z, y), fsdp: 8 (over x, core).
Axes of the slice: x: 4, y: 4, z: 32, core: 2. Of those that a mesh axis runs over, the one named last changes fastest.
Arguments:
- queries: bfloat16 [32768, 3072], P('dp', 'fsdp'), may hold values from -1.4 to 1.4
- key_rows: bfloat16 [32768, 3072], P('dp', 'fsdp'), may hold values from -5 to 5
- values: bfloat16 [32768, 3072], P('dp', 'fsdp'), may hold values from -20 to 20
- log_decay: float32 [32, 32768], P('fsdp', 'dp'), may hold values from -0.8 to 0
- segment_ids: int32 [32768], P('dp'), may hold values from 0 to 63, as said below
- norm_gain: float32 [3072], P('fsdp'), may hold values from 0.5 to 1.5
- grad_out: bfloat16 [32768, 3072], P('dp', 'fsdp'), may hold values from -8 to 8
Outputs:
- attended: bfloat16 [32768, 3072], P('dp', 'fsdp')
- grad_queries: bfloat16 [32768, 3072], P('dp', 'fsdp')
- grad_keys: bfloat16 [32768, 3072], P('dp', 'fsdp')
- grad_values: bfloat16 [32768, 3072], P('dp', 'fsdp')
- grad_gain: float32 [3072], P('fsdp')
Inputs may be any that keep to these rules, and one draw needn't show every extreme that they name: `segment_ids`: each response is one run of consecutive packed tokens; the ids rise by one from response to response and every id is used; every response's length is a multiple of 128 and at most 16384; one response has exactly 16384 tokens.
All inputs are finite; a program needn't handle non-finite values.
Results may differ from a plain program's by a relative error of at most 0.0056.
Values sent between devices are 32-bit elements; how exact they have to be, the bound alone decides.
No kernel may reach another device: no remote copies, remote signals or barrier semaphores. Data moves between devices by JAX's collectives and lax.ppermute only.
A program may use at most 128 MiB of HBM per device.

v0:
```python
from functools import reduce

import jax
import jax.numpy as jnp
from jax import lax
from jax.sharding import PartitionSpec as P

BLOCK = 256


EPSILON = 1e-06
PRECISE = lax.Precision.HIGHEST


def passed_along(value, axis, steps):
    count = lax.axis_size(axis)
    first, last = (max(0, -steps), min(count, count - steps))
    return lax.ppermute(value, axis, [(source, source + steps) for source in range(first, last)])


def block_decays(decay_rows, segment_rows, blocks, width):
    head_count = decay_rows.shape[0]
    cumulative = jnp.cumsum(decay_rows.reshape(head_count, blocks, width), axis=2)
    segment_blk = segment_rows.reshape(blocks, width)
    first_seg = segment_blk[:, 0]
    last_seg = segment_blk[:, -1]
    causal = lax.broadcasted_iota(jnp.int32, (width, width), 0) >= lax.broadcasted_iota(
        jnp.int32, (width, width), 1
    )
    allowed = jnp.logical_and(segment_blk[:, :, None] == segment_blk[:, None, :], causal[None])[
        None
    ]
    gap_decay = cumulative[:, :, :, None] - cumulative[:, :, None, :]
    decay_mask = jnp.where(allowed, jnp.exp(jnp.where(allowed, gap_decay, 0.0)), 0.0)
    lead_decay = jnp.exp(cumulative) * (segment_blk == first_seg[:, None])[None].astype(jnp.float32)
    tail_decay = jnp.exp(cumulative[:, :, -1:] - cumulative) * (segment_blk == last_seg[:, None])[
        None
    ].astype(jnp.float32)
    through = jnp.exp(cumulative[:, :, -1]) * (first_seg == last_seg)[None].astype(jnp.float32)
    return (decay_mask, lead_decay, tail_decay, through, first_seg + 1, last_seg + 1)


def combine_spans(earlier, later):
    earlier_pass, earlier_state, earlier_near, earlier_far = earlier
    later_pass, later_state, later_near, later_far = later
    linked = jnp.logical_or(
        jnp.logical_or(earlier_far == later_near, earlier_far == 0), later_near == 0
    )
    carried = later_pass * linked.astype(jnp.float32)
    merged_state = later_state + carried[:, None, None] * earlier_state
    merged_near = jnp.where(earlier_near == 0, later_near, earlier_near)
    merged_far = jnp.where(later_far == 0, earlier_far, later_far)
    return (earlier_pass * carried, merged_state, merged_near, merged_far)


def offsets_for(span_devices):
    offsets = [1]
    width = 1
    while width < span_devices:
        offsets.append(width)
        width = width * 2
    return offsets


def near_forward(totals, span_devices):
    window_sum = totals
    for index, offset in enumerate(offsets_for(span_devices)):
        shifted = passed_along(
            (window_sum[0], window_sum[1], window_sum[2], window_sum[3]), "dp", offset
        )
        window_sum = shifted if index == 0 else combine_spans(shifted, window_sum)
    return window_sum


def near_backward(totals, span_devices):
    window_sum = totals
    for index, offset in enumerate(offsets_for(span_devices)):
        shifted = passed_along(
            (window_sum[0], window_sum[1], window_sum[2], window_sum[3]), "dp", -offset
        )
        window_sum = shifted if index == 0 else combine_spans(shifted, window_sum)
    return window_sum


def local(queries, key_rows, values, log_decay, segment_ids, norm_gain, grad_out):
    row_count, feature_count = queries.shape
    head_count = log_decay.shape[0]
    head_size = feature_count // head_count
    blocks = row_count // BLOCK
    dp_count = lax.axis_size("dp")
    longest = min(64 * row_count, row_count * dp_count // 2)
    span_devices = (longest - 2) // row_count + 1
    query_b = queries.reshape(blocks, BLOCK, head_count, head_size)
    key_b = key_rows.reshape(blocks, BLOCK, head_count, head_size)
    value_b = values.reshape(blocks, BLOCK, head_count, head_size)
    decay_mask, lead_decay, tail_decay, through, near_tag, far_tag = block_decays(
        log_decay, segment_ids, blocks, BLOCK
    )
    scores = jnp.einsum("bthd,bshd->hbts", query_b, key_b, preferred_element_type=jnp.float32)
    attn_probs = (scores * decay_mask).astype(jnp.bfloat16)
    inner_part = jnp.einsum(
        "hbts,bshd->bthd", attn_probs, value_b, preferred_element_type=jnp.float32
    )
    keyed = (key_b * tail_decay.transpose(1, 2, 0)[..., None]).astype(jnp.bfloat16)
    summary = jnp.einsum("bshd,bshe->bhde", keyed, value_b, preferred_element_type=jnp.float32)
    through_b = through.T
    forward_spans = [(through_b[0], summary[0], near_tag[0], far_tag[0])]
    device_span = reduce(combine_spans, forward_spans)
    before = near_forward(device_span, span_devices)
    running = before
    incoming = [running[1]]
    incoming_tags = [running[3]]
    states_in = jnp.stack(incoming)
    tags_in = jnp.stack(incoming_tags)
    enter = (lead_decay * (tags_in == near_tag).astype(jnp.float32)[None, :, None]).transpose(
        1, 2, 0
    )[..., None]
    outer_part = jnp.einsum(
        "bthd,bhde->bthe", query_b.astype(jnp.float32), states_in, precision=PRECISE
    )
    attention = (inner_part + outer_part * enter).reshape(row_count, feature_count)
    total_width = feature_count * lax.axis_size("fsdp")
    squares = lax.psum(jnp.sum(attention * attention, axis=1), "fsdp")
    inv_rms = lax.rsqrt(squares / total_width + EPSILON)
    normed = attention * inv_rms[:, None]
    attended = (normed * norm_gain[None, :]).astype(jnp.bfloat16)
    grad_float = grad_out.astype(jnp.float32)
    grad_normed = grad_float * norm_gain[None, :]
    dot_terms = lax.psum(jnp.sum(grad_normed * normed, axis=1), "fsdp")
    grad_attn = (
        inv_rms[:, None] * (grad_normed - normed * (dot_terms / total_width)[:, None])
    ).astype(jnp.bfloat16)
    gain_terms = jnp.sum(grad_float * normed, axis=0)
    grad_gain = lax.psum(gain_terms, "dp") * float(row_count * dp_count) ** (-0.5)
    grad_b = grad_attn.reshape(blocks, BLOCK, head_count, head_size)
    score_grads = (
        jnp.einsum("bthd,bshd->hbts", grad_b, value_b, preferred_element_type=jnp.float32)
        * decay_mask
    ).astype(jnp.bfloat16)
    grad_q = jnp.einsum("hbts,bshd->bthd", score_grads, key_b, preferred_element_type=jnp.float32)
    grad_q = (
        grad_q
        + jnp.einsum("bthe,bhde->bthd", grad_b.astype(jnp.float32), states_in, precision=PRECISE)
        * enter
    )
    grad_k = jnp.einsum("hbts,bthd->bshd", score_grads, query_b, preferred_element_type=jnp.float32)
    grad_v = jnp.einsum("hbts,bthd->bshd", attn_probs, grad_b, preferred_element_type=jnp.float32)
    queued = (query_b * lead_decay.transpose(1, 2, 0)[..., None]).astype(jnp.bfloat16)
    back_summary = jnp.einsum("bthd,bthe->bhde", queued, grad_b, preferred_element_type=jnp.float32)
    backward_spans = [(through_b[0], back_summary[0], far_tag[0], near_tag[0])]
    device_back = reduce(combine_spans, backward_spans[::-1])
    from_after = near_backward(device_back, span_devices)
    outgoing = [None] * blocks
    outgoing_tags = [None] * blocks
    running = from_after
    outgoing[0] = running[1]
    outgoing_tags[0] = running[3]
    back_in = jnp.stack(outgoing)
    back_tags = jnp.stack(outgoing_tags)
    leave = (tail_decay * (back_tags == far_tag).astype(jnp.float32)[None, :, None]).transpose(
        1, 2, 0
    )[..., None]
    grad_k = (
        grad_k
        + jnp.einsum("bhde,bshe->bshd", back_in, value_b.astype(jnp.float32), precision=PRECISE)
        * leave
    )
    grad_v = (
        grad_v
        + jnp.einsum("bshd,bhde->bshe", key_b.astype(jnp.float32), back_in, precision=PRECISE)
        * leave
    )
    grad_queries = grad_q.reshape(row_count, feature_count).astype(jnp.bfloat16)
    grad_keys = grad_k.reshape(row_count, feature_count).astype(jnp.bfloat16)
    grad_values = grad_v.reshape(row_count, feature_count).astype(jnp.bfloat16)
    return (attended, grad_queries, grad_keys, grad_values, grad_gain)


def solution(mesh):
    return jax.shard_map(
        local,
        mesh=mesh,
        in_specs=(
            P("dp", "fsdp"),
            P("dp", "fsdp"),
            P("dp", "fsdp"),
            P("fsdp", "dp"),
            P("dp"),
            P("fsdp"),
            P("dp", "fsdp"),
        ),
        out_specs=(P("dp", "fsdp"), P("dp", "fsdp"), P("dp", "fsdp"), P("dp", "fsdp"), P("fsdp")),
        check_vma=False,
    )
```

profile of v0, /device:TPU:54, one launch (start us, length us, event | category | flops | bytes accessed | tf_op | source)
XLA Modules:
  0.0 736.0 jit_solution(16100917038599669727)
XLA Ops:
  17.2 6.1 collective-permute-start.2
  31.3 7.3 collective-permute-start.4
  81.7 6.9 collective-permute-start.12
  106.9 11.5 %collective-permute-start.16 = (s32[]{:T(128)}, s32[]{:T(128)}, u32[]{:S(2)}, u32[]{:S(2)}) collective-permute-start(s32[]{:T(128)} %select_n.81), channel_id=1, source_target_pairs={{0,32},{8,40},{16,48},{24,56},{32,64},{40,72},{48,80},{56,88},{64,... | collective-permute-start | bytes 20 | tf_op jit(solution)/shard_map/ppermute | solution.py:18
  121.6 11.0 %collective-permute-start.15 = (s32[]{:T(128)}, s32[]{:T(128)}, u32[]{:S(2)}, u32[]{:S(2)}) collective-permute-start(s32[]{:T(128)} %select_n.82), channel_id=1, source_target_pairs={{0,64},{8,72},{16,80},{24,88},{32,96},{40,104},{48,112},{56,120},{... | collective-permute-start | bytes 20 | tf_op jit(solution)/shard_map/ppermute | solution.py:18
  138.4 9.2 %collective-permute-start.20 = (s32[]{:T(128)}, s32[]{:T(128)}, u32[]{:S(2)}, u32[]{:S(2)}) collective-permute-start(s32[]{:T(128)} %select_n.83), channel_id=1, source_target_pairs={{0,64},{8,72},{16,80},{24,88},{32,96},{40,104},{48,112},{56,120},{... | collective-permute-start | bytes 20 | tf_op jit(solution)/shard_map/ppermute | solution.py:18
  159.8 12.3 %collective-permute-start.19 = (s32[]{:T(128)}, s32[]{:T(128)}, u32[]{:S(2)}, u32[]{:S(2)}) collective-permute-start(s32[]{:T(128)} %select_n.84), channel_id=1, source_target_pairs={{0,128},{8,136},{16,144},{24,152},{32,160},{40,168},{48,176},{56,1... | collective-permute-start | bytes 20 | tf_op jit(solution)/shard_map/ppermute | solution.py:18
  177.8 12.3 %collective-permute-start.24 = (s32[]{:T(128)}, s32[]{:T(128)}, u32[]{:S(2)}, u32[]{:S(2)}) collective-permute-start(s32[]{:T(128)} %select_n.85), channel_id=1, source_target_pairs={{0,128},{8,136},{16,144},{24,152},{32,160},{40,168},{48,176},{56,1... | collective-permute-start | bytes 20 | tf_op jit(solution)/shard_map/ppermute | solution.py:18
  190.7 15.7 %collective-permute-start.23 = (s32[]{:T(128)}, s32[]{:T(128)}, u32[]{:S(2)}, u32[]{:S(2)}) collective-permute-start(s32[]{:T(128)} %select_n.86), channel_id=1, source_target_pairs={{0,256},{8,264},{16,272},{24,280},{32,288},{40,296},{48,304},{56,3... | collective-permute-start | bytes 20 | tf_op jit(solution)/shard_map/ppermute | solution.py:18
  213.9 7.4 %collective-permute-done.49 = s32[]{:T(128)} collective-permute-done((s32[]{:T(128)}, s32[]{:T(128)}, u32[]{:S(2)}, u32[]{:S(2)}) %collective-permute-start.49) | collective-permute-done | bytes 36 | tf_op jit(solution)/shard_map/ppermute | solution.py:18
  232.6 6.3 collective-permute-start.10
  263.0 8.2 %collective-permute-start.18 = (f32[4]{0:T(128)S(1)}, f32[4]{0:T(128)S(1)}, u32[]{:S(2)}, u32[]{:S(2)}) collective-permute-start(f32[4]{0:T(128)S(1)} %get-tuple-element.43), channel_id=1, source_target_pairs={{0,64},{8,72},{16,80},{24,88},{32,96},{40,104},{48,112},{56,120},{... | collective-permute-start | bytes 56 | tf_op jit(solution)/shard_map/ppermute | solution.py:18
  271.4 7.8 %collective-permute-start.17 = (f32[4,96,96]{2,1,0:T(8,128)S(1)}, f32[4,96,96]{2,1,0:T(8,128)S(1)}, u32[]{:S(2)}, u32[]{:S(2)}) collective-permute-start(f32[4,96,96]{2,1,0:T(8,128)S(1)} %multiply_add_fusion.9), channel_id=1, source_target_pairs={{0,64},{8,72},{16,80},{24,88},{32,96},{40,104},{48,112},{56,120},{... | collective-permute-start | bytes 442376 | tf_op jit(solution)/shard_map/ppermute | solution.py:18
  279.2 6.6 collective-permute-start.22
  285.9 25.7 %collective-permute-start.21 = (f32[4,96,96]{2,1,0:T(8,128)S(1)}, f32[4,96,96]{2,1,0:T(8,128)S(1)}, u32[]{:S(2)}, u32[]{:S(2)}) collective-permute-start(f32[4,96,96]{2,1,0:T(8,128)S(1)} %multiply_add_fusion.8), channel_id=1, source_target_pairs={{0,128},{8,136},{16,144},{24,152},{32,160},{40,168},{48,176},{56,1... | collective-permute-start | bytes 442376 | tf_op jit(solution)/shard_map/ppermute | solution.py:18
  314.9 12.4 %collective-permute-start.25 = (f32[4,96,96]{2,1,0:T(8,128)S(1)}, f32[4,96,96]{2,1,0:T(8,128)S(1)}, u32[]{:S(2)}, u32[]{:S(2)}) collective-permute-start(f32[4,96,96]{2,1,0:T(8,128)S(1)} %multiply_add_fusion.7), channel_id=1, source_target_pairs={{0,256},{8,264},{16,272},{24,280},{32,288},{40,296},{48,304},{56,3... | collective-permute-start | bytes 442376 | tf_op jit(solution)/shard_map/ppermute | solution.py:18
  330.9 10.3 %psum.21 = f32[256]{0:T(256)S(1)} all-reduce(f32[256]{0:T(256)S(1)} %get-tuple-element.58), channel_id=1, replica_groups=mesh['dp'=128,'fsdp'=8] {'fsdp'}, use_global_device_ids=true, to_apply=%region_3.4 | all-reduce | flops 256 | bytes 2048 | tf_op jit(solution)/shard_map/psum | solution.py:123
  342.1 11.0 %psum.22 = f32[256]{0:T(256)S(1)} all-reduce(f32[256]{0:T(256)S(1)} %get-tuple-element.26), channel_id=1, replica_groups=mesh['dp'=128,'fsdp'=8] {'fsdp'}, use_global_device_ids=true, to_apply=%region_5.6 | all-reduce | flops 256 | bytes 2048 | tf_op jit(solution)/shard_map/psum | solution.py:129
  363.1 7.4 %collective-permute-start.31 = (f32[4,96,96]{2,1,0:T(8,128)S(1)}, f32[4,96,96]{2,1,0:T(8,128)S(1)}, u32[]{:S(2)}, u32[]{:S(2)}) collective-permute-start(f32[4,96,96]{2,1,0:T(8,128)S(1)} %collective-permute-done.26), channel_id=1, source_target_pairs={{8,0},{16,8},{24,16},{32,24},{40,32},{48,40},{56,48},{64,56},{72,6... | collective-permute-start | bytes 442376 | tf_op jit(solution)/shard_map/ppermute | solution.py:18
  374.6 6.4 collective-permute-start.35
  392.2 276.5 %psum.23 = f32[384]{0:T(512)S(1)} all-reduce(f32[384]{0:T(512)S(1)} %get-tuple-element.25), channel_id=1, replica_groups=mesh['dp'=128,'fsdp'=8] {'dp'}, use_global_device_ids=true, to_apply=%region_7.8 | all-reduce | flops 384 | bytes 3072 | tf_op jit(solution)/shard_map/psum | solution.py:134
  670.6 10.5 %collective-permute-done.43 = f32[4,96,96]{2,1,0:T(8,128)S(1)} collective-permute-done((f32[4,96,96]{2,1,0:T(8,128)S(1)}, f32[4,96,96]{2,1,0:T(8,128)S(1)}, u32[]{:S(2)}, u32[]{:S(2)}) %collective-permute-start.43) | collective-permute-done | bytes 147488 | tf_op jit(solution)/shard_map/ppermute | solution.py:18
  682.8 11.4 %collective-permute-done.47 = f32[4,96,96]{2,1,0:T(8,128)S(1)} collective-permute-done((f32[4,96,96]{2,1,0:T(8,128)S(1)}, f32[4,96,96]{2,1,0:T(8,128)S(1)}, u32[]{:S(2)}, u32[]{:S(2)}) %collective-permute-start.47) | collective-permute-done | bytes 147488 | tf_op jit(solution)/shard_map/ppermute | solution.py:18
  695.8 37.8 %collective-permute-done.51 = f32[4,96,96]{2,1,0:T(8,128)S(1)} collective-permute-done((f32[4,96,96]{2,1,0:T(8,128)S(1)}, f32[4,96,96]{2,1,0:T(8,128)S(1)}, u32[]{:S(2)}, u32[]{:S(2)}) %collective-permute-start.51) | collective-permute-done | bytes 147488 | tf_op jit(solution)/shard_map/ppermute | solution.py:18
  (157 shorter events, 153.5 us)
Async XLA Ops:
  7.0 131.4 %collective-permute-start.27 = (f32[4]{0:T(128)S(1)}, f32[4]{0:T(128)S(1)}, u32[]{:S(2)}, u32[]{:S(2)}) collective-permute-start(f32[4]{0:T(128)S(1)} %exponential_multiply_fusion.2), channel_id=1, source_target_pairs={{8,0},{16,8},{24,16},{32,24},{40,32},{48,40},{56,48},{64,56},{72,6... | collective-permute-start | bytes 56 | tf_op jit(solution)/shard_map/ppermute | solution.py:18
  9.4 138.3 %collective-permute-start.1 = (f32[4]{0:T(128)S(1)}, f32[4]{0:T(128)S(1)}, u32[]{:S(2)}, u32[]{:S(2)}) collective-permute-start(f32[4]{0:T(128)S(1)} %exponential_multiply_fusion.2), channel_id=1, source_target_pairs={{0,8},{8,16},{16,24},{24,32},{32,40},{40,48},{48,56},{56,64},{64,7... | collective-permute-start | bytes 56 | tf_op jit(solution)/shard_map/ppermute | solution.py:18
  17.2 22.0 %collective-permute-start.2 = (s32[]{:T(128)}, s32[]{:T(128)}, u32[]{:S(2)}, u32[]{:S(2)}) collective-permute-start(s32[]{:T(128)} %bitcast.14), channel_id=1, source_target_pairs={{0,8},{8,16},{16,24},{24,32},{32,40},{40,48},{48,56},{56,64},{64,7... | collective-permute-start | bytes 20 | tf_op jit(solution)/shard_map/ppermute | solution.py:18
  50.9 25.0 %collective-permute-start.8 = (s32[]{:T(128)}, s32[]{:T(128)}, u32[]{:S(2)}, u32[]{:S(2)}) collective-permute-start(s32[]{:T(128)} %collective-permute-done.4), channel_id=1, source_target_pairs={{0,8},{8,16},{16,24},{24,32},{32,40},{40,48},{48,56},{56,64},{64,7... | collective-permute-start | bytes 20 | tf_op jit(solution)/shard_map/ppermute | solution.py:18
  58.8 22.9 %collective-permute-start.38 = (s32[]{:T(128)}, s32[]{:T(128)}, u32[]{:S(2)}, u32[]{:S(2)}) collective-permute-start(s32[]{:T(128)} %select_n.90), channel_id=1, source_target_pairs={{16,0},{24,8},{32,16},{40,24},{48,32},{56,40},{64,48},{72,56},{80,... | collective-permute-start | bytes 20 | tf_op jit(solution)/shard_map/ppermute | solution.py:18
  64.9 25.0 %collective-permute-start.7 = (s32[]{:T(128)}, s32[]{:T(128)}, u32[]{:S(2)}, u32[]{:S(2)}) collective-permute-start(s32[]{:T(128)} %select_n.78), channel_id=1, source_target_pairs={{0,16},{8,24},{16,32},{24,40},{32,48},{40,56},{48,64},{56,72},{64,... | collective-permute-start | bytes 20 | tf_op jit(solution)/shard_map/ppermute | solution.py:18
  81.7 20.7 %collective-permute-start.12 = (s32[]{:T(128)}, s32[]{:T(128)}, u32[]{:S(2)}, u32[]{:S(2)}) collective-permute-start(s32[]{:T(128)} %select_n.79), channel_id=1, source_target_pairs={{0,16},{8,24},{16,32},{24,40},{32,48},{40,56},{48,64},{56,72},{64,... | collective-permute-start | bytes 20 | tf_op jit(solution)/shard_map/ppermute | solution.py:18
  93.7 25.9 %collective-permute-start.11 = (s32[]{:T(128)}, s32[]{:T(128)}, u32[]{:S(2)}, u32[]{:S(2)}) collective-permute-start(s32[]{:T(128)} %select_n.80), channel_id=1, source_target_pairs={{0,32},{8,40},{16,48},{24,56},{32,64},{40,72},{48,80},{56,88},{64,... | collective-permute-start | bytes 20 | tf_op jit(solution)/shard_map/ppermute | solution.py:18
  106.9 28.9 %collective-permute-start.16 = (s32[]{:T(128)}, s32[]{:T(128)}, u32[]{:S(2)}, u32[]{:S(2)}) collective-permute-start(s32[]{:T(128)} %select_n.81), channel_id=1, source_target_pairs={{0,32},{8,40},{16,48},{24,56},{32,64},{40,72},{48,80},{56,88},{64,... | collective-permute-start | bytes 20 | tf_op jit(solution)/shard_map/ppermute | solution.py:18
  119.6 31.1 %collective-permute-start.46 = (s32[]{:T(128)}, s32[]{:T(128)}, u32[]{:S(2)}, u32[]{:S(2)}) collective-permute-start(s32[]{:T(128)} %select_n.94), channel_id=1, source_target_pairs={{64,0},{72,8},{80,16},{88,24},{96,32},{104,40},{112,48},{120,56},{... | collective-permute-start | bytes 20 | tf_op jit(solution)/shard_map/ppermute | solution.py:18
  121.6 36.4 %collective-permute-start.15 = (s32[]{:T(128)}, s32[]{:T(128)}, u32[]{:S(2)}, u32[]{:S(2)}) collective-permute-start(s32[]{:T(128)} %select_n.82), channel_id=1, source_target_pairs={{0,64},{8,72},{16,80},{24,88},{32,96},{40,104},{48,112},{56,120},{... | collective-permute-start | bytes 20 | tf_op jit(solution)/shard_map/ppermute | solution.py:18
  135.9 24.0 %collective-permute-start.41 = (s32[]{:T(128)}, s32[]{:T(128)}, u32[]{:S(2)}, u32[]{:S(2)}) collective-permute-start(s32[]{:T(128)} %select_n.93), channel_id=1, source_target_pairs={{64,0},{72,8},{80,16},{88,24},{96,32},{104,40},{112,48},{120,56},{... | collective-permute-start | bytes 20 | tf_op jit(solution)/shard_map/ppermute | solution.py:18
  138.4 36.8 %collective-permute-start.20 = (s32[]{:T(128)}, s32[]{:T(128)}, u32[]{:S(2)}, u32[]{:S(2)}) collective-permute-start(s32[]{:T(128)} %select_n.83), channel_id=1, source_target_pairs={{0,64},{8,72},{16,80},{24,88},{32,96},{40,104},{48,112},{56,120},{... | collective-permute-start | bytes 20 | tf_op jit(solution)/shard_map/ppermute | solution.py:18
  147.7 82.9 %collective-permute-start.32 = (f32[4]{0:T(128)S(1)}, f32[4]{0:T(128)S(1)}, u32[]{:S(2)}, u32[]{:S(2)}) collective-permute-start(f32[4]{0:T(128)S(1)} %collective-permute-done.27), channel_id=1, source_target_pairs={{8,0},{16,8},{24,16},{32,24},{40,32},{48,40},{56,48},{64,56},{72,6... | collective-permute-start | bytes 56 | tf_op jit(solution)/shard_map/ppermute | solution.py:18
  150.8 81.8 %collective-permute-start.6 = (f32[4]{0:T(128)S(1)}, f32[4]{0:T(128)S(1)}, u32[]{:S(2)}, u32[]{:S(2)}) collective-permute-start(f32[4]{0:T(128)S(1)} %collective-permute-done.1), channel_id=1, source_target_pairs={{0,8},{8,16},{16,24},{24,32},{32,40},{40,48},{48,56},{56,64},{64,7... | collective-permute-start | bytes 56 | tf_op jit(solution)/shard_map/ppermute | solution.py:18
  158.0 49.1 %collective-permute-start.50 = (s32[]{:T(128)}, s32[]{:T(128)}, u32[]{:S(2)}, u32[]{:S(2)}) collective-permute-start(s32[]{:T(128)} %select_n.96), channel_id=1, source_target_pairs={{128,0},{136,8},{144,16},{152,24},{160,32},{168,40},{176,48},{184,... | collective-permute-start | bytes 20 | tf_op jit(solution)/shard_map/ppermute | solution.py:18
  177.8 34.2 %collective-permute-start.24 = (s32[]{:T(128)}, s32[]{:T(128)}, u32[]{:S(2)}, u32[]{:S(2)}) collective-permute-start(s32[]{:T(128)} %select_n.85), channel_id=1, source_target_pairs={{0,128},{8,136},{16,144},{24,152},{32,160},{40,168},{48,176},{56,1... | collective-permute-start | bytes 20 | tf_op jit(solution)/shard_map/ppermute | solution.py:18
  190.7 22.5 %collective-permute-start.23 = (s32[]{:T(128)}, s32[]{:T(128)}, u32[]{:S(2)}, u32[]{:S(2)}) collective-permute-start(s32[]{:T(128)} %select_n.86), channel_id=1, source_target_pairs={{0,256},{8,264},{16,272},{24,280},{32,288},{40,296},{48,304},{56,3... | collective-permute-start | bytes 20 | tf_op jit(solution)/shard_map/ppermute | solution.py:18
  253.4 73.9 %collective-permute-start.44 = (f32[4]{0:T(128)S(1)}, f32[4]{0:T(128)S(1)}, u32[]{:S(2)}, u32[]{:S(2)}) collective-permute-start(f32[4]{0:T(128)S(1)} %get-tuple-element.31), channel_id=1, source_target_pairs={{64,0},{72,8},{80,16},{88,24},{96,32},{104,40},{112,48},{120,56},{... | collective-permute-start | bytes 56 | tf_op jit(solution)/shard_map/ppermute | solution.py:18
  279.2 32.5 %collective-permute-start.22 = (f32[4]{0:T(128)S(1)}, f32[4]{0:T(128)S(1)}, u32[]{:S(2)}, u32[]{:S(2)}) collective-permute-start(f32[4]{0:T(128)S(1)} %get-tuple-element.41), channel_id=1, source_target_pairs={{0,128},{8,136},{16,144},{24,152},{32,160},{40,168},{48,176},{56,1... | collective-permute-start | bytes 56 | tf_op jit(solution)/shard_map/ppermute | solution.py:18
  285.9 28.9 %collective-permute-start.21 = (f32[4,96,96]{2,1,0:T(8,128)S(1)}, f32[4,96,96]{2,1,0:T(8,128)S(1)}, u32[]{:S(2)}, u32[]{:S(2)}) collective-permute-start(f32[4,96,96]{2,1,0:T(8,128)S(1)} %multiply_add_fusion.8), channel_id=1, source_target_pairs={{0,128},{8,136},{16,144},{24,152},{32,160},{40,168},{48,176},{56,1... | collective-permute-start | bytes 442376 | tf_op jit(solution)/shard_map/ppermute | solution.py:18
  327.3 30.9 %collective-permute-start.48 = (f32[4]{0:T(128)S(1)}, f32[4]{0:T(128)S(1)}, u32[]{:S(2)}, u32[]{:S(2)}) collective-permute-start(f32[4]{0:T(128)S(1)} %get-tuple-element.29), channel_id=1, source_target_pairs={{128,0},{136,8},{144,16},{152,24},{160,32},{168,40},{176,48},{184,... | collective-permute-start | bytes 56 | tf_op jit(solution)/shard_map/ppermute | solution.py:18
  384.8 283.8 %collective-permute-start.39 = (f32[4,96,96]{2,1,0:T(8,128)S(1)}, f32[4,96,96]{2,1,0:T(8,128)S(1)}, u32[]{:S(2)}, u32[]{:S(2)}) collective-permute-start(f32[4,96,96]{2,1,0:T(8,128)S(1)} %multiply_add_fusion.4), channel_id=1, source_target_pairs={{32,0},{40,8},{48,16},{56,24},{64,32},{72,40},{80,48},{88,56},{96,... | collective-permute-start | bytes 442376 | tf_op jit(solution)/shard_map/ppermute | solution.py:18
  694.3 39.3 %collective-permute-start.51 = (f32[4,96,96]{2,1,0:T(8,128)S(1)}, f32[4,96,96]{2,1,0:T(8,128)S(1)}, u32[]{:S(2)}, u32[]{:S(2)}) collective-permute-start(f32[4,96,96]{2,1,0:T(8,128)S(1)} %multiply_add_fusion.1), channel_id=1, source_target_pairs={{256,0},{264,8},{272,16},{280,24},{288,32},{296,40},{304,48},{312,... | collective-permute-start | bytes 442376 | tf_op jit(solution)/shard_map/ppermute | solution.py:18
  (33 other events, 406.2 us)
where the time goes:
time: 738 us; the launch traced here: 736 us
  blocking collectives  298 us (40%)
  starting transfers between devices  288 us (39%)
  waiting for transfers between devices  87.8 us (12%)
  between operations  44.4 us (6%)
  local copies, waits for them, and re-layouts  9.63 us (1%)
    ppermute x52, starting transfers between devices, passed_along(): lax.ppermute(value, axis, [(source, source + steps) for source in range(f...  288 us
    psum x1, blocking collectives, local(): lax.psum(gain_terms, 'dp') * float(row_count * dp_count) ** (-0.5)  276 us
    ppermute x52, waiting for transfers between devices, passed_along(): lax.ppermute(value, axis, [(source, source + steps) for source in range(f...  87.8 us
  transfers between devices with their start and end apart: 52, of which 11 were waited for; matrix products, arithmetic and copies ran while one was open for 1% of the time, Pallas kernels for 0%

commit v1 on v0

v1 whole, which is shorter than its diff:
```python
import functools

import jax
import jax.numpy as jnp
from jax import lax
from jax.experimental import pallas as pl
from jax.experimental.pallas import tpu as pltpu
from jax.sharding import Mesh
from jax.sharding import PartitionSpec as P

BLOCK = 256
EPSILON = 1e-06
PRECISE = lax.Precision.HIGHEST
PASS, NEAR, FAR, GAIN = 96, 97, 98, 99


def links(near, far):
    return [None] + [(far[k - 1] == near[k]).astype(jnp.float32) for k in range(1, len(near))]


def columns(ref, count):
    picked = [[ref[k, :, lane : lane + 1] for k in range(count)] for lane in (PASS, NEAR, FAR)]
    return picked


def total_kernel(backward, pieces_ref, out_ref):
    count, rows, lanes = pieces_ref.shape
    order = list(range(count))[::-1] if backward else list(range(count))
    passes, near, far = columns(pieces_ref, count)
    if backward:
        near, far = far, near
    lane = lax.broadcasted_iota(jnp.int32, (rows, lanes), 1)
    running = pieces_ref[order[0]]
    gain = running
    through = passes[order[0]]
    for before, k in zip(order[:-1], order[1:]):
        piece = pieces_ref[k]
        carried = passes[k] * (far[before] == near[k]).astype(jnp.float32)
        running = piece + carried * running
        through = through * carried
        gain = gain + piece
    first, last = order[0], order[-1]
    out = jnp.where(lane < PASS, running, gain)
    out = jnp.where(lane == PASS, through, out)
    out = jnp.where(lane == NEAR, near[first], out)
    out = jnp.where(lane == FAR, far[last], out)
    for g in range(out_ref.shape[0]):
        out_ref[g] = out


def prefix_kernel(backward, mine_ref, pieces_ref, groups_ref, out_ref):
    count, rows, lanes = pieces_ref.shape
    group_count = groups_ref.shape[0]
    mine = mine_ref[0]
    lane = lax.broadcasted_iota(jnp.int32, (rows, lanes), 1)
    group_order = list(range(group_count))[::-1] if backward else list(range(group_count))
    running = jnp.zeros((rows, lanes), jnp.float32)
    gain = jnp.zeros((rows, lanes), jnp.float32)
    last_far = jnp.full((rows, 1), -1.0, jnp.float32)
    entering = running
    entering_far = last_far
    for g in group_order:
        here = mine == g
        entering = jnp.where(here, running, entering)
        entering_far = jnp.where(here, last_far, entering_far)
        piece = groups_ref[g]
        joined = (last_far == piece[:, NEAR : NEAR + 1]).astype(jnp.float32)
        running = piece + (piece[:, PASS : PASS + 1] * joined) * running
        gain = gain + piece
        last_far = piece[:, FAR : FAR + 1]
    order = list(range(count))[::-1] if backward else list(range(count))
    passes, near, far = columns(pieces_ref, count)
    if backward:
        near, far = far, near
    state = entering
    before_far = entering_far
    for k in order:
        joined = (before_far == near[k]).astype(jnp.float32)
        state = state * joined
        out_ref[k] = jnp.where(lane < PASS, state, gain)
        state = pieces_ref[k] + passes[k] * state
        before_far = far[k]


def scan_states(summary, through, near, far, gain, backward):
    head_count, rows, cols = summary.shape
    group = lax.axis_size("near")
    parts = group // head_count
    sub = rows // parts
    extra = jnp.stack(
        [
            jnp.broadcast_to(through[:, None], (head_count, rows)),
            jnp.broadcast_to(near.astype(jnp.float32), (head_count, rows)),
            jnp.broadcast_to(far.astype(jnp.float32), (head_count, rows)),
            gain,
        ],
        axis=2,
    )
    extra = jnp.pad(extra, ((0, 0), (0, 0), (0, 128 - cols - 4)))
    pieces = jnp.concatenate([summary, extra], axis=2).reshape(group, sub, 128)
    pieces = lax.all_to_all(pieces, "near", 0, 0, tiled=True)
    group_count = lax.axis_size("wide")
    total = pl.pallas_call(
        functools.partial(total_kernel, backward),
        out_shape=jax.ShapeDtypeStruct((group_count, sub, 128), jnp.float32),
        name="group_total",
    )(pieces)
    groups = lax.all_to_all(total, "wide", 0, 0, tiled=True)
    mine = lax.axis_index("wide").astype(jnp.int32).reshape(1)
    states = pl.pallas_call(
        functools.partial(prefix_kernel, backward),
        out_shape=jax.ShapeDtypeStruct((group, sub, 128), jnp.float32),
        in_specs=[
            pl.BlockSpec(memory_space=pltpu.SMEM),
            pl.BlockSpec(memory_space=pltpu.VMEM),
            pl.BlockSpec(memory_space=pltpu.VMEM),
        ],
        name="group_prefix",
    )(mine, pieces, groups)
    states = lax.all_to_all(states, "near", 0, 0, tiled=True).reshape(head_count, rows, 128)
    return states[:, :, :cols], states[:, :, GAIN]


def local(queries, key_rows, values, log_decay, segment_ids, norm_gain, grad_out):
    row_count, feature_count = queries.shape
    head_count = log_decay.shape[0]
    head_size = feature_count // head_count
    dp_count = lax.axis_size("wide") * lax.axis_size("near")
    query_b = queries.reshape(row_count, head_count, head_size)
    key_b = key_rows.reshape(row_count, head_count, head_size)
    value_b = values.reshape(row_count, head_count, head_size)
    cumulative = jnp.cumsum(log_decay, axis=1)
    near, far = segment_ids[0], segment_ids[-1]
    causal = lax.broadcasted_iota(jnp.int32, (BLOCK, BLOCK), 0) >= lax.broadcasted_iota(
        jnp.int32, (BLOCK, BLOCK), 1
    )
    allowed = jnp.logical_and(segment_ids[:, None] == segment_ids[None, :], causal)[None]
    gap = cumulative[:, :, None] - cumulative[:, None, :]
    decay_mask = jnp.where(allowed, jnp.exp(jnp.where(allowed, gap, 0.0)), 0.0)
    lead = jnp.exp(cumulative) * (segment_ids == near)[None].astype(jnp.float32)
    tail = jnp.exp(cumulative[:, -1:] - cumulative) * (segment_ids == far)[None].astype(jnp.float32)
    through = jnp.exp(cumulative[:, -1]) * (near == far).astype(jnp.float32)
    lead = lead.T[..., None]
    tail = tail.T[..., None]
    keyed = (key_b * tail).astype(jnp.bfloat16)
    summary = jnp.einsum("shd,she->hde", keyed, value_b, preferred_element_type=jnp.float32)
    zeros = jnp.zeros((head_count, head_size), jnp.float32)
    state_in, _ = scan_states(summary, through, near, far, zeros, False)
    scores = jnp.einsum("thd,shd->hts", query_b, key_b, preferred_element_type=jnp.float32)
    attn_probs = (scores * decay_mask).astype(jnp.bfloat16)
    inner = jnp.einsum("hts,shd->thd", attn_probs, value_b, preferred_element_type=jnp.float32)
    outer = jnp.einsum("thd,hde->the", query_b.astype(jnp.float32), state_in, precision=PRECISE)
    attention = (inner + outer * lead).reshape(row_count, feature_count)
    grad_float = grad_out.astype(jnp.float32)
    grad_normed = grad_float * norm_gain[None, :]
    sums = jnp.stack(
        [jnp.sum(attention * attention, axis=1), jnp.sum(grad_normed * attention, axis=1)]
    )
    fsdp = lax.axis_size("fsdp")
    sums = lax.all_to_all(
        jnp.broadcast_to(sums[None], (fsdp, 2, row_count)), "fsdp", 0, 0, tiled=True
    ).sum(axis=0)
    width = feature_count * fsdp
    inv_rms = lax.rsqrt(sums[0] / width + EPSILON)
    dots = sums[1] * inv_rms / width
    normed = attention * inv_rms[:, None]
    attended = (normed * norm_gain[None, :]).astype(jnp.bfloat16)
    grad_attn = (inv_rms[:, None] * (grad_normed - normed * dots[:, None])).astype(jnp.bfloat16)
    gain_terms = jnp.sum(grad_float * normed, axis=0).reshape(head_count, head_size)
    grad_b = grad_attn.reshape(row_count, head_count, head_size)
    queued = (query_b * lead).astype(jnp.bfloat16)
    back_summary = jnp.einsum("thd,the->hde", queued, grad_b, preferred_element_type=jnp.float32)
    back_in, gain = scan_states(back_summary, through, near, far, gain_terms, True)
    grad_gain = gain.reshape(feature_count) * float(row_count * dp_count) ** (-0.5)
    score_grads = (
        jnp.einsum("thd,shd->hts", grad_b, value_b, preferred_element_type=jnp.float32) * decay_mask
    ).astype(jnp.bfloat16)
    grad_q = jnp.einsum("hts,shd->thd", score_grads, key_b, preferred_element_type=jnp.float32)
    grad_q = (
        grad_q
        + jnp.einsum("the,hde->thd", grad_b.astype(jnp.float32), state_in, precision=PRECISE) * lead
    )
    grad_k = jnp.einsum("hts,thd->shd", score_grads, query_b, preferred_element_type=jnp.float32)
    grad_v = jnp.einsum("hts,thd->shd", attn_probs, grad_b, preferred_element_type=jnp.float32)
    grad_k = (
        grad_k
        + jnp.einsum("hde,she->shd", back_in, value_b.astype(jnp.float32), precision=PRECISE) * tail
    )
    grad_v = (
        grad_v
        + jnp.einsum("shd,hde->she", key_b.astype(jnp.float32), back_in, precision=PRECISE) * tail
    )
    shape = (row_count, feature_count)
    return (
        attended,
        grad_q.reshape(shape).astype(jnp.bfloat16),
        grad_k.reshape(shape).astype(jnp.bfloat16),
        grad_v.reshape(shape).astype(jnp.bfloat16),
        grad_gain,
    )


def solution(mesh):
    dp_count, fsdp_count = mesh.devices.shape
    near_count = 16
    fine = Mesh(
        mesh.devices.reshape(dp_count // near_count, near_count, fsdp_count),
        ("wide", "near", "fsdp"),
    )
    dp = ("wide", "near")
    return jax.shard_map(
        local,
        mesh=fine,
        in_specs=(
            P(dp, "fsdp"),
            P(dp, "fsdp"),
            P(dp, "fsdp"),
            P("fsdp", dp),
            P(dp),
            P("fsdp"),
            P(dp, "fsdp"),
        ),
        out_specs=(P(dp, "fsdp"), P(dp, "fsdp"), P(dp, "fsdp"), P(dp, "fsdp"), P("fsdp")),
        check_vma=False,
    )
```

time: 738 us -> 175 us (0.24)
  the two profiles are of different devices: /device:TPU:54 before, /device:TPU:8 now
where the time goes in v1:
time: 175 us; the launch traced here: 174 us
  blocking collectives  77 us (44%)
  waiting for transfers between devices  37.1 us (21%)
  starting transfers between devices  30.2 us (17%)
  local copies, waits for them, and re-layouts  10.3 us (6%)
  Pallas kernels  8.58 us (5%)
  other arithmetic  3.88 us (2%)
  matrix products  3.78 us (2%)
  between operations  3.44 us (2%)
    all_to_all x2, blocking collectives, scan_states(): pieces = lax.all_to_all(pieces, 'near', 0, 0, tiled=True)  37.5 us
    all_to_all x1, blocking collectives, scan_states(): groups = lax.all_to_all(total, 'wide', 0, 0, tiled=True)  30 us
    all_to_all x1, waiting for transfers between devices, scan_states(): groups = lax.all_to_all(total, 'wide', 0, 0, tiled=True)  25.4 us
    all_to_all x1, starting transfers between devices, scan_states(): groups = lax.all_to_all(total, 'wide', 0, 0, tiled=True)  18.4 us
    all_to_all x2, waiting for transfers between devices, scan_states(): lax.all_to_all(states, 'near', 0, 0, tiled=True)  11.8 us
    all_to_all x2, starting transfers between devices, scan_states(): lax.all_to_all(states, 'near', 0, 0, tiled=True)  11.7 us
    all_to_all x1, blocking collectives, local(): lax.all_to_all(jnp.broadcast_to(sums[None], (fsdp, 2, row_count)), 'fsdp'...  9.46 us
    unnamed x24, local copies, waits for them, and re-layouts  7.37 us
  transfers between devices with their start and end apart: 3, of which 3 were waited for; matrix products, arithmetic and copies ran while one was open for 2% of the time, Pallas kernels for 0%

profile of v1, /device:TPU:8, one launch (start us, length us, event | category | flops | bytes accessed | tf_op | source)
XLA Modules:
  0.0 174.2 jit_solution(15590333888018650350)
XLA Ops:
  0.6 1.3 fusion.34
  2.0 0.7 copy-done.4
  2.7 1.3 compare_convert_fusion.1
  6.6 1.2 reduce-window.6
  8.4 1.1 copy.105
  10.4 24.4 %all_to_all.35.pieces_ref = f32[16,24,128]{2,1,0:T(8,128)} all-to-all(f32[16,24,128]{2,1,0:T(8,128)S(1)} %bitcast.126), channel_id=1, replica_groups=mesh['wide'=8,'near'=16,'fsdp'=8] {'near'}, dimensions={0} | all-to-all | bytes 393216 | tf_op jit(solution)/shard_map/all_to_all | solution.py:101
  34.8 1.8 %group_total.2 = f32[8,24,128]{2,1,0:T(8,128)} custom-call(f32[16,24,128]{2,1,0:T(8,128)} %all_to_all.35.pieces_ref), custom_call_target="tpu_custom_call" | custom-call | tf_op jit(solution)/shard_map/group_total/pallas_call | solution.py:103
  36.6 18.4 %all-to-all-start.1 = ((f32[8,24,128]{2,1,0:T(8,128)}), f32[8,24,128]{2,1,0:T(8,128)S(1)}, u32[]{:S(2)}, u32[]{:S(2)}) async-start(f32[8,24,128]{2,1,0:T(8,128)} %group_total.2), calls=%async_computation.1 | async-start | bytes 196608 | tf_op jit(solution)/shard_map/all_to_all | solution.py:108
  55.1 25.4 %all-to-all-done.1.groups_ref = f32[8,24,128]{2,1,0:T(8,128)S(1)} async-done(((f32[8,24,128]{2,1,0:T(8,128)}), f32[8,24,128]{2,1,0:T(8,128)S(1)}, u32[]{:S(2)}, u32[]{:S(2)}) %all-to-all-start.1) | async-done | bytes 98336 | tf_op jit(solution)/shard_map/all_to_all | solution.py:108
  81.1 2.4 %group_prefix.2 = f32[16,24,128]{2,1,0:T(8,128)} custom-call(s32[1]{0:T(128)} %bitcast.5.mine_ref, f32[16,24,128]{2,1,0:T(8,128)} %all_to_all.35.pieces_ref, f32[8,24,128]{2,1,0:T(8,128)} %copy-done), custom_call_target="tpu_custom_call" | custom-call | tf_op jit(solution)/shard_map/group_prefix/pallas_call | solution.py:110
  83.5 6.2 %all-to-all-start.2 = ((f32[16,24,128]{2,1,0:T(8,128)}), f32[16,24,128]{2,1,0:T(8,128)S(1)}, u32[]{:S(2)}, u32[]{:S(2)}) async-start(f32[16,24,128]{2,1,0:T(8,128)} %group_prefix.2), calls=%async_computation.2 | async-start | bytes 393216 | tf_op jit(solution)/shard_map/all_to_all | solution.py:120
  89.8 0.8 copy-done.3
  91.3 6.4 %all-to-all-done.2 = f32[16,24,128]{2,1,0:T(8,128)S(1)} async-done(((f32[16,24,128]{2,1,0:T(8,128)}), f32[16,24,128]{2,1,0:T(8,128)S(1)}, u32[]{:S(2)}, u32[]{:S(2)}) %all-to-all-start.2) | async-done | bytes 196640 | tf_op jit(solution)/shard_map/all_to_all | solution.py:120
  99.0 9.5 %all_to_all.36 = f32[8,2,256]{2,1,0:T(2,128)S(1)} all-to-all(f32[8,2,256]{2,1,0:T(2,128)S(1)} %broadcast_in_dim.20), channel_id=1, replica_groups=mesh['wide'=8,'near'=16,'fsdp'=8] {'fsdp'}, dimensions={0} | all-to-all | bytes 32768 | tf_op jit(solution)/shard_map/all_to_all | solution.py:160
  109.4 13.1 %all_to_all.37.pieces_ref = f32[16,24,128]{2,1,0:T(8,128)} all-to-all(f32[16,24,128]{2,1,0:T(8,128)S(1)} %bitcast.127), channel_id=1, replica_groups=mesh['wide'=8,'near'=16,'fsdp'=8] {'near'}, dimensions={0} | all-to-all | bytes 393216 | tf_op jit(solution)/shard_map/all_to_all | solution.py:101
  122.5 1.8 %group_total.3 = f32[8,24,128]{2,1,0:T(8,128)} custom-call(f32[16,24,128]{2,1,0:T(8,128)} %all_to_all.37.pieces_ref), custom_call_target="tpu_custom_call" | custom-call | tf_op jit(solution)/shard_map/group_total/pallas_call | solution.py:103
  124.4 30.0 %all_to_all.38.groups_ref = f32[8,24,128]{2,1,0:T(8,128)} all-to-all(f32[8,24,128]{2,1,0:T(8,128)} %group_total.3), channel_id=1, replica_groups=mesh['wide'=8,'near'=16,'fsdp'=8] {'wide'}, dimensions={0} | all-to-all | bytes 196608 | tf_op jit(solution)/shard_map/all_to_all | solution.py:108
  154.4 2.5 %group_prefix.3 = f32[16,24,128]{2,1,0:T(8,128)} custom-call(s32[1]{0:T(128)} %bitcast.5.mine_ref, f32[16,24,128]{2,1,0:T(8,128)} %all_to_all.37.pieces_ref, f32[8,24,128]{2,1,0:T(8,128)} %all_to_all.38.groups_ref), custom_call_target="tpu_custom_call" | custom-call | tf_op jit(solution)/shard_map/group_prefix/pallas_call | solution.py:110
  156.8 5.6 %all-to-all-start.6 = ((f32[16,24,128]{2,1,0:T(8,128)}), f32[16,24,128]{2,1,0:T(8,128)S(1)}, u32[]{:S(2)}, u32[]{:S(2)}) async-start(f32[16,24,128]{2,1,0:T(8,128)} %group_prefix.3), calls=%async_computation.6 | async-start | bytes 393216 | tf_op jit(solution)/shard_map/all_to_all | solution.py:120
  163.5 0.8 copy.117
  164.3 0.8 copy.116
  165.1 5.4 %all-to-all-done.6 = f32[16,24,128]{2,1,0:T(8,128)S(1)} async-done(((f32[16,24,128]{2,1,0:T(8,128)}), f32[16,24,128]{2,1,0:T(8,128)S(1)}, u32[]{:S(2)}, u32[]{:S(2)}) %all-to-all-start.6) | async-done | bytes 196640 | tf_op jit(solution)/shard_map/all_to_all | solution.py:120
  171.7 0.8 copy.119
  172.7 0.8 copy.118
  (58 shorter events, 8.2 us)
Async XLA Ops:
  2.0 0.7 copy-start.4
  2.6 3.9 %copy-start.6 = (f32[4,256]{1,0:T(4,128)S(1)}, f32[4,256]{1,0:T(4,128)}, u32[]{:S(2)}) copy-start(f32[4,256]{1,0:T(4,128)} %param.10) | copy-start | bytes 12292
  8.4 1.1 copy-start.1
  36.6 43.8 %all-to-all-start.1 = ((f32[8,24,128]{2,1,0:T(8,128)}), f32[8,24,128]{2,1,0:T(8,128)S(1)}, u32[]{:S(2)}, u32[]{:S(2)}) async-start(f32[8,24,128]{2,1,0:T(8,128)} %group_total.2), calls=%async_computation.1 | async-start | bytes 196608 | tf_op jit(solution)/shard_map/all_to_all | solution.py:108
  80.4 0.6 copy-start
  83.5 6.2 %copy-start.2 = (bf16[256,384]{1,0:T(8,128)(2,1)S(1)}, bf16[256,384]{1,0:T(8,128)(2,1)}, u32[]{:S(2)}) copy-start(bf16[256,384]{1,0:T(8,128)(2,1)} %param.7) | copy-start | bytes 589828
  83.5 14.3 %all-to-all-start.2 = ((f32[16,24,128]{2,1,0:T(8,128)}), f32[16,24,128]{2,1,0:T(8,128)S(1)}, u32[]{:S(2)}, u32[]{:S(2)}) async-start(f32[16,24,128]{2,1,0:T(8,128)} %group_prefix.2), calls=%async_computation.2 | async-start | bytes 393216 | tf_op jit(solution)/shard_map/all_to_all | solution.py:120
  89.7 0.9 copy-start.3
  98.1 0.7 copy-start.5
  156.8 13.7 %all-to-all-start.6 = ((f32[16,24,128]{2,1,0:T(8,128)}), f32[16,24,128]{2,1,0:T(8,128)S(1)}, u32[]{:S(2)}, u32[]{:S(2)}) async-start(f32[16,24,128]{2,1,0:T(8,128)} %group_prefix.3), calls=%async_computation.6 | async-start | bytes 393216 | tf_op jit(solution)/shard_map/all_to_all | solution.py:120

commit v2 on v1

v2 whole, which is shorter than its diff:
```python
import functools

import jax
import jax.numpy as jnp
from jax import lax
from jax.experimental import pallas as pl
from jax.experimental.pallas import tpu as pltpu
from jax.sharding import Mesh
from jax.sharding import PartitionSpec as P

BLOCK = 256
EPSILON = 1e-06
PRECISE = lax.Precision.HIGHEST
PASS, NEAR, FAR, GAIN = 96, 97, 98, 99


HEADS, HEAD, TILE = 4, 96, 128
SUB = 24
STARTS = tuple(HEAD * h % TILE for h in range(HEADS))
WINDOWS = tuple((HEAD * h // TILE, (HEAD * h + HEAD - 1) // TILE + 1) for h in range(HEADS))


def on_chip(kernel, outs, operands, name, flops=0, exps=0):
    placed, specs, moved = [], [], 0
    for x in operands:
        if x.dtype == jnp.int32:
            placed.append(x)
            specs.append(pl.BlockSpec(memory_space=pltpu.SMEM))
        else:
            placed.append(pltpu.with_memory_space_constraint(x, pltpu.VMEM))
            specs.append(pl.BlockSpec(memory_space=pltpu.VMEM))
            moved += x.size * x.dtype.itemsize
    for out in outs:
        moved += out.size * out.dtype.itemsize if hasattr(out, "size") else 0
    return pl.pallas_call(
        kernel,
        out_shape=outs,
        in_specs=specs,
        out_specs=[pl.BlockSpec(memory_space=pltpu.VMEM) for _ in outs],
        cost_estimate=pl.CostEstimate(
            flops=flops, bytes_accessed=moved, transcendentals=exps
        ),
        compiler_params=pltpu.CompilerParams(vmem_limit_bytes=40 * 1024 * 1024),
        name=name,
    )(*placed)


def dot(a, b, over_a=1, over_b=0):
    return lax.dot_general(
        a, b, (((over_a,), (over_b,)), ((), ())), preferred_element_type=jnp.float32
    )


def pick_heads(parts, tile, rows):
    lane = lax.broadcasted_iota(jnp.int32, (rows, TILE), 1) + tile * TILE
    inside = [h for h in range(HEADS) if WINDOWS[h][0] <= tile < WINDOWS[h][1]]
    out = parts[inside[-1]]
    for h in inside[:-1][::-1]:
        out = jnp.where(lane < HEAD * (h + 1), parts[h], out)
    return out


def over_features(cols, first, rows):
    spread = [jnp.broadcast_to(cols[:, first + h : first + h + 1], (rows, TILE)) for h in range(HEADS)]
    return jnp.concatenate([pick_heads(spread, c, rows) for c in range(3)], axis=1)


def only_head(x, h):
    low, high = WINDOWS[h]
    x = x[:, low * TILE : high * TILE]
    lane = lax.broadcasted_iota(jnp.int32, x.shape, 1) + low * TILE
    inside = jnp.logical_and(lane >= HEAD * h, lane < HEAD * (h + 1))
    return jnp.where(inside, x, jnp.zeros_like(x))


def write_pieces(left, right, rows_ref, gain, out_ref):
    full = dot(left, right, 0, 0)
    lane = lax.broadcasted_iota(jnp.int32, (HEAD, TILE), 1)
    last = BLOCK - 1
    same, near, far = (rows_ref[r : r + 1, last:] for r in (4, 5, 6))
    for h in range(HEADS):
        low, high = WINDOWS[h]
        tiles = [full[HEAD * h : HEAD * (h + 1), TILE * c : TILE * (c + 1)] for c in range(low, high)]
        state = tiles[0] if len(tiles) == 1 else jnp.where(lane >= STARTS[h], tiles[0], tiles[1])
        if STARTS[h]:
            state = pltpu.roll(state, TILE - STARTS[h], 1)
        through = jnp.exp(rows_ref[h : h + 1, last:]) * same
        state = jnp.where(lane < HEAD, state, through)
        state = jnp.where(lane == NEAR, near, state)
        state = jnp.where(lane == FAR, far, state)
        state = jnp.where(lane == GAIN, 0.0 if gain is None else gain[HEAD * h : HEAD * (h + 1)], state)
        for i in range(HEAD // SUB):
            out_ref[h * (HEAD // SUB) + i] = state[i * SUB : (i + 1) * SUB]


def read_states(pieces_ref):
    lane = lax.broadcasted_iota(jnp.int32, (HEAD, TILE), 1)
    zero = jnp.zeros((HEAD, TILE), jnp.float32)
    parts = HEAD // SUB
    bands = []
    for h in range(HEADS):
        state = jnp.concatenate([pieces_ref[h * parts + i] for i in range(parts)], axis=0)
        state = jnp.where(lane < HEAD, state, 0.0)
        if STARTS[h]:
            state = pltpu.roll(state, STARTS[h], 1)
        low, high = WINDOWS[h]
        tiles = [zero] * 3
        if high - low == 1:
            tiles[low] = state
        else:
            tiles[low] = jnp.where(lane >= STARTS[h], state, 0.0)
            tiles[low + 1] = jnp.where(lane >= STARTS[h], 0.0, state)
        bands.append(jnp.concatenate(tiles, axis=1))
    whole = jnp.concatenate(bands, axis=0)
    high = whole.astype(jnp.bfloat16)
    return high, (whole - high.astype(jnp.float32)).astype(jnp.bfloat16)


def summary_kernel(segment_ref, decay_ref, key_ref, value_ref, pieces_ref, rows_ref, cols_ref):
    near, far = segment_ref[0], segment_ref[BLOCK - 1]
    same = (near == far).astype(jnp.float32)
    earlier = lax.broadcasted_iota(jnp.int32, (BLOCK, BLOCK), 0) <= lax.broadcasted_iota(
        jnp.int32, (BLOCK, BLOCK), 1
    )
    decay = decay_ref[...]
    decay = jnp.concatenate([decay, decay], axis=0)
    cumulative = jnp.dot(
        decay, earlier.astype(jnp.float32), precision=PRECISE, preferred_element_type=jnp.float32
    )
    row = lax.broadcasted_iota(jnp.int32, (8, BLOCK), 0)
    first_half = lax.broadcasted_iota(jnp.int32, (8, BLOCK), 1) < BLOCK // 2
    last = cumulative[:, BLOCK - 1 :]
    in_near = jnp.where(first_half, 1.0, same)
    in_far = jnp.where(first_half, same, 1.0)
    decays = jnp.where(
        row < HEADS, jnp.exp(cumulative) * in_near, jnp.exp(last - cumulative) * in_far
    )
    tags = jnp.where(row == 4, same, jnp.where(row == 5, near.astype(jnp.float32), far.astype(jnp.float32)))
    rows_ref[...] = jnp.where(row < HEADS, cumulative, tags)
    cols = jnp.transpose(jnp.concatenate([decays, cumulative], axis=0))
    cols_ref[...] = cols
    keyed = key_ref[...].astype(jnp.float32) * over_features(cols, 4, BLOCK)
    write_pieces(keyed.astype(jnp.bfloat16), value_ref[...], rows_ref, None, pieces_ref)


def decay_masks(rows_ref, cols_ref):
    t = lax.broadcasted_iota(jnp.int32, (BLOCK, BLOCK), 0)
    s = lax.broadcasted_iota(jnp.int32, (BLOCK, BLOCK), 1)
    half = BLOCK // 2
    together = jnp.logical_or((t < half) == (s < half), rows_ref[4:5, :] > 0.5)
    allowed = jnp.logical_and(t >= s, together)
    for h in range(HEADS):
        gap = cols_ref[:, 8 + h : 9 + h] - rows_ref[h : h + 1, :]
        yield h, jnp.exp(jnp.where(allowed, gap, -1e30))


def times_heads(weights, x, over):
    tiles = []
    for c in range(3):
        column = x[:, c * TILE : (c + 1) * TILE]
        parts = [
            dot(weights[h], column, over, 0) if WINDOWS[h][0] <= c < WINDOWS[h][1] else None
            for h in range(HEADS)
        ]
        tiles.append(pick_heads(parts, c, BLOCK))
    return jnp.concatenate(tiles, axis=1)


def inside_kernel(rows_ref, cols_ref, query_ref, key_ref, value_ref, probs_ref, inner_ref):
    query, key = query_ref[...], key_ref[...]
    weights = []
    for h, mask in decay_masks(rows_ref, cols_ref):
        low, high = WINDOWS[h]
        scores = dot(only_head(query, h), key[:, low * TILE : high * TILE], 1, 1)
        weights.append((scores * mask).astype(jnp.bfloat16))
        probs_ref[h] = weights[h]
    inner_ref[...] = times_heads(weights, value_ref[...], 1)


def attention_kernel(
    states_ref, inner_ref, cols_ref, query_ref, grad_ref, gain_ref, attention_ref, sums_ref
):
    high, low = read_states(states_ref)
    query = query_ref[...]
    outer = dot(query, high) + dot(query, low)
    attention = inner_ref[...] + outer * over_features(cols_ref[...], 0, BLOCK)
    attention_ref[...] = attention
    squares = attention * attention
    products = grad_ref[...].astype(jnp.float32) * gain_ref[...] * attention
    sums = []
    for x in (squares, products):
        x = x[:, :TILE] + x[:, TILE : 2 * TILE] + x[:, 2 * TILE :]
        sums.append(jnp.sum(jnp.transpose(x), axis=0, keepdims=True))
    sums = jnp.concatenate(sums, axis=0)
    for k in range(sums_ref.shape[0]):
        sums_ref[k] = sums


def gradient_kernel(
    width, sums_ref, attention_ref, grad_ref, gain_ref, rows_ref, cols_ref, query_ref,
    grad_attn_ref, inv_ref, pieces_ref,
):
    sums = sums_ref[0]
    for k in range(1, sums_ref.shape[0]):
        sums = sums + sums_ref[k]
    inv = lax.rsqrt(sums[0:1] / width + EPSILON)
    dots = sums[1:2] * inv / width
    row = lax.broadcasted_iota(jnp.int32, (8, BLOCK), 0)
    both = jnp.transpose(jnp.where(row == 0, inv, dots))
    inv_ref[...] = both
    inv, dots = both[:, 0:1], both[:, 1:2]
    normed = attention_ref[...] * inv
    grad = grad_ref[...].astype(jnp.float32)
    grad_attn = (inv * (grad * gain_ref[...] - normed * dots)).astype(jnp.bfloat16)
    grad_attn_ref[...] = grad_attn
    gain = jnp.sum(grad * normed, axis=0, keepdims=True)
    gain = jnp.transpose(jnp.broadcast_to(gain, (8, gain.shape[1])))
    queued = query_ref[...].astype(jnp.float32) * over_features(cols_ref[...], 0, BLOCK)
    write_pieces(queued.astype(jnp.bfloat16), grad_attn, rows_ref, gain[:, 0:1], pieces_ref)


def inside_back_kernel(
    rows_ref, cols_ref, query_ref, key_ref, value_ref, probs_ref, grad_attn_ref, states_ref,
    attention_ref, inv_ref, gain_ref,
    grad_query_ref, part_key_ref, part_value_ref, attended_ref,
):
    grad_attn, value = grad_attn_ref[...], value_ref[...]
    weights = []
    for h, mask in decay_masks(rows_ref, cols_ref):
        low, high = WINDOWS[h]
        grads = dot(only_head(grad_attn, h), value[:, low * TILE : high * TILE], 1, 1)
        weights.append((grads * mask).astype(jnp.bfloat16))
    high, low = read_states(states_ref)
    outer = dot(grad_attn, high, 1, 1) + dot(grad_attn, low, 1, 1)
    grad_query = times_heads(weights, key_ref[...], 1) + outer * over_features(cols_ref[...], 0, BLOCK)
    grad_query_ref[...] = grad_query.astype(jnp.bfloat16)
    part_key_ref[...] = times_heads(weights, query_ref[...], 0)
    part_value_ref[...] = times_heads([probs_ref[h] for h in range(HEADS)], grad_attn, 0)
    attended = attention_ref[...] * inv_ref[:, 0:1] * gain_ref[...]
    attended_ref[...] = attended.astype(jnp.bfloat16)


def last_kernel(
    scale, states_ref, cols_ref, key_ref, value_ref, part_key_ref, part_value_ref,
    grad_key_ref, grad_value_ref, grad_gain_ref,
):
    high, low = read_states(states_ref)
    tail = over_features(cols_ref[...], 4, BLOCK)
    key, value = key_ref[...], value_ref[...]
    outer = dot(value, high, 1, 1) + dot(value, low, 1, 1)
    grad_key_ref[...] = (part_key_ref[...] + outer * tail).astype(jnp.bfloat16)
    outer = dot(key, high) + dot(key, low)
    grad_value_ref[...] = (part_value_ref[...] + outer * tail).astype(jnp.bfloat16)
    count = states_ref.shape[0]
    gain = jnp.concatenate([states_ref[k] for k in range(count)], axis=0)
    grad_gain_ref[...] = jnp.transpose(gain)[GAIN : GAIN + 1] * scale


def scan_states(pieces, backward):
    group, sub, lanes = pieces.shape
    pieces = lax.all_to_all(pieces, "near", 0, 0, tiled=True)
    group_count = lax.axis_size("wide")
    (total,) = on_chip(
        functools.partial(total_kernel, backward),
        [pltpu.VMEM((group_count, sub, lanes), jnp.float32)],
        [pieces],
        "group_total",
    )
    groups = lax.all_to_all(total, "wide", 0, 0, tiled=True)
    mine = lax.axis_index("wide").astype(jnp.int32).reshape(1)
    (states,) = on_chip(
        functools.partial(prefix_kernel, backward),
        [pltpu.VMEM((group, sub, lanes), jnp.float32)],
        [mine, pieces, groups],
        "group_prefix",
    )
    return lax.all_to_all(states, "near", 0, 0, tiled=True)


def local(queries, key_rows, values, log_decay, segment_ids, norm_gain, grad_out):
    tokens, features = queries.shape
    group = lax.axis_size("near")
    dp_count = lax.axis_size("wide") * group
    fsdp = lax.axis_size("fsdp")
    full = (tokens, features)
    mxu = 2 * tokens * tokens * HEAD * HEADS
    pieces, rows, cols = on_chip(
        summary_kernel,
        [
            pltpu.VMEM((group, SUB, TILE), jnp.float32),
            pltpu.VMEM((8, tokens), jnp.float32),
            pltpu.VMEM((tokens, 16), jnp.float32),
        ],
        [segment_ids, log_decay, key_rows, values],
        "summary",
        flops=mxu,
    )
    probs, inner = on_chip(
        inside_kernel,
        [pltpu.VMEM((HEADS, tokens, tokens), jnp.bfloat16), pltpu.VMEM(full, jnp.float32)],
        [rows, cols, queries, key_rows, values],
        "inside",
        flops=4 * mxu,
        exps=HEADS * tokens * tokens,
    )
    state_in = scan_states(pieces, False)
    gain_row = norm_gain.reshape(1, features)
    attention, sums = on_chip(
        attention_kernel,
        [pltpu.VMEM(full, jnp.float32), pltpu.VMEM((fsdp, 2, tokens), jnp.float32)],
        [state_in, inner, cols, queries, grad_out, gain_row],
        "attention",
        flops=2 * mxu,
    )
    sums = lax.all_to_all(sums, "fsdp", 0, 0, tiled=True)
    grad_attn, inv, back_pieces = on_chip(
        functools.partial(gradient_kernel, features * fsdp),
        [
            pltpu.VMEM(full, jnp.bfloat16),
            pltpu.VMEM((tokens, 8), jnp.float32),
            pltpu.VMEM((group, SUB, TILE), jnp.float32),
        ],
        [sums, attention, grad_out, gain_row, rows, cols, queries],
        "gradient",
        flops=mxu,
    )
    grad_queries, part_key, part_value, attended = on_chip(
        inside_back_kernel,
        [
            jax.ShapeDtypeStruct(full, jnp.bfloat16),
            pltpu.VMEM(full, jnp.float32),
            pltpu.VMEM(full, jnp.float32),
            jax.ShapeDtypeStruct(full, jnp.bfloat16),
        ],
        [rows, cols, queries, key_rows, values, probs, grad_attn, state_in, attention, inv, gain_row],
        "inside_back",
        flops=8 * mxu,
        exps=HEADS * tokens * tokens,
    )
    back_in = scan_states(back_pieces, True)
    grad_keys, grad_values, grad_gain = on_chip(
        functools.partial(last_kernel, float(tokens * dp_count) ** (-0.5)),
        [
            jax.ShapeDtypeStruct(full, jnp.bfloat16),
            jax.ShapeDtypeStruct(full, jnp.bfloat16),
            jax.ShapeDtypeStruct((1, features), jnp.float32),
        ],
        [back_in, cols, key_rows, values, part_key, part_value],
        "last",
        flops=4 * mxu,
    )
    return (attended, grad_queries, grad_keys, grad_values, grad_gain.reshape(features))


def columns(ref, count):
    picked = [[ref[k, :, lane : lane + 1] for k in range(count)] for lane in (PASS, NEAR, FAR)]
    return picked


def total_kernel(backward, pieces_ref, out_ref):
    count, rows, lanes = pieces_ref.shape
    order = list(range(count))[::-1] if backward else list(range(count))
    passes, near, far = columns(pieces_ref, count)
    if backward:
        near, far = far, near
    lane = lax.broadcasted_iota(jnp.int32, (rows, lanes), 1)
    running = pieces_ref[order[0]]
    gain = running
    through = passes[order[0]]
    for before, k in zip(order[:-1], order[1:]):
        piece = pieces_ref[k]
        carried = passes[k] * (far[before] == near[k]).astype(jnp.float32)
        running = piece + carried * running
        through = through * carried
        gain = gain + piece
    first, last = order[0], order[-1]
    out = jnp.where(lane < PASS, running, gain)
    out = jnp.where(lane == PASS, through, out)
    out = jnp.where(lane == NEAR, near[first], out)
    out = jnp.where(lane == FAR, far[last], out)
    for g in range(out_ref.shape[0]):
        out_ref[g] = out


def prefix_kernel(backward, mine_ref, pieces_ref, groups_ref, out_ref):
    count, rows, lanes = pieces_ref.shape
    group_count = groups_ref.shape[0]
    mine = mine_ref[0]
    lane = lax.broadcasted_iota(jnp.int32, (rows, lanes), 1)
    group_order = list(range(group_count))[::-1] if backward else list(range(group_count))
    running = jnp.zeros((rows, lanes), jnp.float32)
    gain = jnp.zeros((rows, lanes), jnp.float32)
    last_far = jnp.full((rows, 1), -1.0, jnp.float32)
    entering = running
    entering_far = last_far
    for g in group_order:
        here = mine == g
        entering = jnp.where(here, running, entering)
        entering_far = jnp.where(here, last_far, entering_far)
        piece = groups_ref[g]
        joined = (last_far == piece[:, NEAR : NEAR + 1]).astype(jnp.float32)
        running = piece + (piece[:, PASS : PASS + 1] * joined) * running
        gain = gain + piece
        last_far = piece[:, FAR : FAR + 1]
    order = list(range(count))[::-1] if backward else list(range(count))
    passes, near, far = columns(pieces_ref, count)
    if backward:
        near, far = far, near
    state = entering
    before_far = entering_far
    for k in order:
        joined = (before_far == near[k]).astype(jnp.float32)
        state = state * joined
        out_ref[k] = jnp.where(lane < PASS, state, gain)
        state = pieces_ref[k] + passes[k] * state
        before_far = far[k]


def solution(mesh):
    dp_count, fsdp_count = mesh.devices.shape
    near_count = 16
    fine = Mesh(
        mesh.devices.reshape(dp_count // near_count, near_count, fsdp_count),
        ("wide", "near", "fsdp"),
    )
    dp = ("wide", "near")
    return jax.shard_map(
        local,
        mesh=fine,
        in_specs=(
            P(dp, "fsdp"),
            P(dp, "fsdp"),
            P(dp, "fsdp"),
            P("fsdp", dp),
            P(dp),
            P("fsdp"),
            P(dp, "fsdp"),
        ),
        out_specs=(P(dp, "fsdp"), P(dp, "fsdp"), P(dp, "fsdp"), P(dp, "fsdp"), P("fsdp")),
        check_vma=False,
    )
```

time: 175 us -> 160 us (0.914)
  the two profiles are of different devices: /device:TPU:8 before, /device:TPU:2 now
where the time goes in v2:
time: 160 us; the launch traced here: 159 us
  blocking collectives  67.7 us (42%)
  waiting for transfers between devices  42.5 us (27%)
  starting transfers between devices  33.3 us (21%)
  Pallas kernels  11.3 us (7%)
  local copies, waits for them, and re-layouts  3.24 us (2%)
    all_to_all x2, blocking collectives, scan_states(): pieces = lax.all_to_all(pieces, 'near', 0, 0, tiled=True)  30.5 us
    all_to_all x1, blocking collectives, scan_states(): groups = lax.all_to_all(total, 'wide', 0, 0, tiled=True)  28.6 us
    all_to_all x1, waiting for transfers between devices, scan_states(): groups = lax.all_to_all(total, 'wide', 0, 0, tiled=True)  26 us
    all_to_all x1, starting transfers between devices, scan_states(): groups = lax.all_to_all(total, 'wide', 0, 0, tiled=True)  25.6 us
    all_to_all x2, waiting for transfers between devices, scan_states(): return lax.all_to_all(states, 'near', 0, 0, tiled=True)  16.5 us
    pallas_call x10, Pallas kernels, on_chip(): pl.pallas_call(kernel, out_shape=outs, in_specs=specs, out_specs=[pl.Bloc...  11.3 us
    all_to_all x1, blocking collectives, local(): sums = lax.all_to_all(sums, 'fsdp', 0, 0, tiled=True)  8.53 us
    all_to_all x2, starting transfers between devices, scan_states(): return lax.all_to_all(states, 'near', 0, 0, tiled=True)  7.64 us
  transfers between devices with their start and end apart: 3, of which 3 were waited for; matrix products, arithmetic and copies ran while one was open for 0% of the time, Pallas kernels for 1%

profile of v2, /device:TPU:2, one launch (start us, length us, event | category | flops | bytes accessed | tf_op | source)
XLA Modules:
  0.0 159.4 jit_solution(2184260452232626334)
XLA Ops:
  0.6 0.9 copy-done.1
  1.6 0.9 copy-done.3
  2.5 0.7 copy-done.6
  3.2 0.7 copy-done.7
  3.9 1.7 %summary.1 = (f32[16,24,128]{2,1,0:T(8,128)S(1)}, f32[8,256]{1,0:T(8,128)S(1)}, f32[256,16]{1,0:T(8,128)S(1)}) custom-call(s32[256]{0:T(256)S(1)} %copy-done.7, f32[4,256]{1,0:T(4,128)S(1)} %copy-done.6, bf16[256,384]{1,0:T(8,128)(2,1)S(1)} %copy-done.1, bf16[256,384]{1,0:T(8,128)(2,1)S(1)} %copy-done.3), custom_call_target="tpu_custom_call" | custom-call | flops 50331648 | bytes 397312 | tf_op jit(solution)/shard_map/summary/pallas_call | solution.py:35
  5.6 18.1 %all_to_all.35.pieces_ref = f32[16,24,128]{2,1,0:T(8,128)S(1)} all-to-all(f32[16,24,128]{2,1,0:T(8,128)S(1)} %get-tuple-element.25), channel_id=1, replica_groups=mesh['wide'=8,'near'=16,'fsdp'=8] {'near'}, dimensions={0} | all-to-all | bytes 393216 | tf_op jit(solution)/shard_map/all_to_all | solution.py:261
  23.6 0.9 group_total.2
  24.5 25.6 %all-to-all-start.1 = ((f32[8,24,128]{2,1,0:T(8,128)}), f32[8,24,128]{2,1,0:T(8,128)S(1)}, u32[]{:S(2)}, u32[]{:S(2)}) async-start(f32[8,24,128]{2,1,0:T(8,128)} %group_total.2), calls=%async_computation.1 | async-start | bytes 196608 | tf_op jit(solution)/shard_map/all_to_all | solution.py:269
  50.2 26.0 %all-to-all-done.1.groups_ref = f32[8,24,128]{2,1,0:T(8,128)S(1)} async-done(((f32[8,24,128]{2,1,0:T(8,128)}), f32[8,24,128]{2,1,0:T(8,128)S(1)}, u32[]{:S(2)}, u32[]{:S(2)}) %all-to-all-start.1) | async-done | bytes 98336 | tf_op jit(solution)/shard_map/all_to_all | solution.py:269
  76.2 1.5 group_prefix.2
  77.8 4.1 %all-to-all-start.2 = ((f32[16,24,128]{2,1,0:T(8,128)}), f32[16,24,128]{2,1,0:T(8,128)S(1)}, u32[]{:S(2)}, u32[]{:S(2)}) async-start(f32[16,24,128]{2,1,0:T(8,128)} %group_prefix.2), calls=%async_computation.2 | async-start | bytes 393216 | tf_op jit(solution)/shard_map/all_to_all | solution.py:277
  82.0 0.6 inside.1
  82.5 8.8 %all-to-all-done.2.states_ref = f32[16,24,128]{2,1,0:T(8,128)S(1)} async-done(((f32[16,24,128]{2,1,0:T(8,128)}), f32[16,24,128]{2,1,0:T(8,128)S(1)}, u32[]{:S(2)}, u32[]{:S(2)}) %all-to-all-start.2) | async-done | bytes 196640 | tf_op jit(solution)/shard_map/all_to_all | solution.py:277
  91.4 0.6 attention.1
  92.0 8.5 %all_to_all.36.sums_ref = f32[8,2,256]{2,1,0:T(2,128)S(1)} all-to-all(f32[8,2,256]{2,1,0:T(2,128)S(1)} %get-tuple-element.27), channel_id=1, replica_groups=mesh['wide'=8,'near'=16,'fsdp'=8] {'fsdp'}, dimensions={0} | all-to-all | bytes 32768 | tf_op jit(solution)/shard_map/all_to_all | solution.py:315
  100.5 1.0 gradient.1
  101.5 12.5 %all_to_all.37.pieces_ref = f32[16,24,128]{2,1,0:T(8,128)S(1)} all-to-all(f32[16,24,128]{2,1,0:T(8,128)S(1)} %get-tuple-element.33), channel_id=1, replica_groups=mesh['wide'=8,'near'=16,'fsdp'=8] {'near'}, dimensions={0} | all-to-all | bytes 393216 | tf_op jit(solution)/shard_map/all_to_all | solution.py:261
  114.3 28.6 %all_to_all.38.groups_ref = f32[8,24,128]{2,1,0:T(8,128)S(1)} all-to-all(f32[8,24,128]{2,1,0:T(8,128)S(1)} %group_total.3), channel_id=1, replica_groups=mesh['wide'=8,'near'=16,'fsdp'=8] {'wide'}, dimensions={0} | all-to-all | bytes 196608 | tf_op jit(solution)/shard_map/all_to_all | solution.py:269
  142.9 1.5 group_prefix.3
  144.4 3.5 %all-to-all-start.6 = ((f32[16,24,128]{2,1,0:T(8,128)}), f32[16,24,128]{2,1,0:T(8,128)S(1)}, u32[]{:S(2)}, u32[]{:S(2)}) async-start(f32[16,24,128]{2,1,0:T(8,128)} %group_prefix.3), calls=%async_computation.6 | async-start | bytes 393216 | tf_op jit(solution)/shard_map/all_to_all | solution.py:277
  148.0 1.8 %inside_back.1 = (bf16[256,384]{1,0:T(8,128)(2,1)}, f32[256,384]{1,0:T(8,128)S(1)}, f32[256,384]{1,0:T(8,128)S(1)}, bf16[256,384]{1,0:T(8,128)(2,1)}) custom-call(f32[8,256]{1,0:T(8,128)S(1)} %get-tuple-element.22.rows_ref, f32[256,16]{1,0:T(8,128)S(1)} %get-tuple-element.23.cols_ref, bf16[256,384]{1,0:T(8,128)(2,1)S(1)} %copy-done, ...), custom_call_target="tpu_custom_call" | custom-call | flops 402653184 | bytes 2328064 | tf_op jit(solution)/shard_map/inside_back/pallas_call | solution.py:35
  149.7 7.6 %all-to-all-done.6.states_ref = f32[16,24,128]{2,1,0:T(8,128)S(1)} async-done(((f32[16,24,128]{2,1,0:T(8,128)}), f32[16,24,128]{2,1,0:T(8,128)S(1)}, u32[]{:S(2)}, u32[]{:S(2)}) %all-to-all-start.6) | async-done | bytes 196640 | tf_op jit(solution)/shard_map/all_to_all | solution.py:277
  157.4 1.4 last.1
  158.8 0.6 reduce
  (16 shorter events, 0.3 us)
Async XLA Ops:
  0.6 0.9 copy-start.1
  1.6 0.9 copy-start.3
  2.5 0.7 copy-start.6
  3.2 0.7 copy-start.7
  24.5 51.7 %all-to-all-start.1 = ((f32[8,24,128]{2,1,0:T(8,128)}), f32[8,24,128]{2,1,0:T(8,128)S(1)}, u32[]{:S(2)}, u32[]{:S(2)}) async-start(f32[8,24,128]{2,1,0:T(8,128)} %group_total.2), calls=%async_computation.1 | async-start | bytes 196608 | tf_op jit(solution)/shard_map/all_to_all | solution.py:269
  76.2 5.7 %copy-start.8 = (f32[384]{0:T(512)S(1)}, f32[384]{0:T(512)}, u32[]{:S(2)}) copy-start(f32[384]{0:T(512)} %param.12) | copy-start | bytes 4612
  76.2 5.7 %copy-start.4 = (bf16[256,384]{1,0:T(8,128)(2,1)S(1)}, bf16[256,384]{1,0:T(8,128)(2,1)}, u32[]{:S(2)}) copy-start(bf16[256,384]{1,0:T(8,128)(2,1)} %value_ref.7) | copy-start | bytes 589828
  77.8 4.2 %copy-start = (bf16[256,384]{1,0:T(8,128)(2,1)S(1)}, bf16[256,384]{1,0:T(8,128)(2,1)}, u32[]{:S(2)}) copy-start(bf16[256,384]{1,0:T(8,128)(2,1)} %query_ref.7) | copy-start | bytes 589828
  77.8 4.2 %copy-start.2 = (bf16[256,384]{1,0:T(8,128)(2,1)S(1)}, bf16[256,384]{1,0:T(8,128)(2,1)}, u32[]{:S(2)}) copy-start(bf16[256,384]{1,0:T(8,128)(2,1)} %key_ref.7) | copy-start | bytes 589828
  77.8 13.6 %all-to-all-start.2 = ((f32[16,24,128]{2,1,0:T(8,128)}), f32[16,24,128]{2,1,0:T(8,128)S(1)}, u32[]{:S(2)}, u32[]{:S(2)}) async-start(f32[16,24,128]{2,1,0:T(8,128)} %group_prefix.2), calls=%async_computation.2 | async-start | bytes 393216 | tf_op jit(solution)/shard_map/all_to_all | solution.py:277
  82.0 9.4 %copy-start.5 = (bf16[256,384]{1,0:T(8,128)(2,1)S(1)}, bf16[256,384]{1,0:T(8,128)(2,1)}, u32[]{:S(2)}) copy-start(bf16[256,384]{1,0:T(8,128)(2,1)} %grad_ref.3) | copy-start | bytes 589828
  144.4 12.9 %all-to-all-start.6 = ((f32[16,24,128]{2,1,0:T(8,128)}), f32[16,24,128]{2,1,0:T(8,128)S(1)}, u32[]{:S(2)}, u32[]{:S(2)}) async-start(f32[16,24,128]{2,1,0:T(8,128)} %group_prefix.3), calls=%async_computation.6 | async-start | bytes 393216 | tf_op jit(solution)/shard_map/all_to_all | solution.py:277

commit v3 on v2

--- a/solution.py
+++ b/solution.py
@@ -20,16 +20,13 @@
 WINDOWS = tuple((HEAD * h // TILE, (HEAD * h + HEAD - 1) // TILE + 1) for h in range(HEADS))
 
 
-def on_chip(kernel, outs, operands, name, flops=0, exps=0):
+def on_chip(kernel, outs, operands, name, flops=0, exps=0, held_in=pltpu.VMEM):
     placed, specs, moved = [], [], 0
     for x in operands:
-        if x.dtype == jnp.int32:
-            placed.append(x)
-            specs.append(pl.BlockSpec(memory_space=pltpu.SMEM))
-        else:
-            placed.append(pltpu.with_memory_space_constraint(x, pltpu.VMEM))
-            specs.append(pl.BlockSpec(memory_space=pltpu.VMEM))
-            moved += x.size * x.dtype.itemsize
+        placed.append(pltpu.with_memory_space_constraint(x, held_in))
+        inside = pltpu.SMEM if x.dtype == jnp.int32 else pltpu.VMEM
+        specs.append(pl.BlockSpec(memory_space=inside))
+        moved += x.size * x.dtype.itemsize
     for out in outs:
         moved += out.size * out.dtype.itemsize if hasattr(out, "size") else 0
     return pl.pallas_call(
@@ -253,7 +250,7 @@
     grad_value_ref[...] = (part_value_ref[...] + outer * tail).astype(jnp.bfloat16)
     count = states_ref.shape[0]
     gain = jnp.concatenate([states_ref[k] for k in range(count)], axis=0)
-    grad_gain_ref[...] = jnp.transpose(gain)[GAIN : GAIN + 1] * scale
+    grad_gain_ref[...] = (jnp.transpose(gain)[GAIN : GAIN + 1] * scale).reshape(gain.shape[0])
 
 
 def scan_states(pieces, backward):
@@ -267,11 +264,10 @@
         "group_total",
     )
     groups = lax.all_to_all(total, "wide", 0, 0, tiled=True)
-    mine = lax.axis_index("wide").astype(jnp.int32).reshape(1)
     (states,) = on_chip(
         functools.partial(prefix_kernel, backward),
         [pltpu.VMEM((group, sub, lanes), jnp.float32)],
-        [mine, pieces, groups],
+        [pieces, groups],
         "group_prefix",
     )
     return lax.all_to_all(states, "near", 0, 0, tiled=True)
@@ -294,6 +290,7 @@
         [segment_ids, log_decay, key_rows, values],
         "summary",
         flops=mxu,
+        held_in=pltpu.HBM,
     )
     probs, inner = on_chip(
         inside_kernel,
@@ -343,13 +340,13 @@
         [
             jax.ShapeDtypeStruct(full, jnp.bfloat16),
             jax.ShapeDtypeStruct(full, jnp.bfloat16),
-            jax.ShapeDtypeStruct((1, features), jnp.float32),
+            jax.ShapeDtypeStruct((features,), jnp.float32),
         ],
         [back_in, cols, key_rows, values, part_key, part_value],
         "last",
         flops=4 * mxu,
     )
-    return (attended, grad_queries, grad_keys, grad_values, grad_gain.reshape(features))
+    return (attended, grad_queries, grad_keys, grad_values, grad_gain)
 
 
 def columns(ref, count):
@@ -382,10 +379,10 @@
         out_ref[g] = out
 
 
-def prefix_kernel(backward, mine_ref, pieces_ref, groups_ref, out_ref):
+def prefix_kernel(backward, pieces_ref, groups_ref, out_ref):
     count, rows, lanes = pieces_ref.shape
     group_count = groups_ref.shape[0]
-    mine = mine_ref[0]
+    mine = lax.axis_index("wide")
     lane = lax.broadcasted_iota(jnp.int32, (rows, lanes), 1)
     group_order = list(range(group_count))[::-1] if backward else list(range(group_count))
     running = jnp.zeros((rows, lanes), jnp.float32)

time: 160 us -> 156 us (0.975)
  blocking collectives: 67.7 us -> 119 us
  waiting for transfers between devices: 42.5 us -> 16.5 us
  starting transfers between devices: 33.3 us -> 7.64 us
  local copies, waits for them, and re-layouts: 3.24 us -> 0.02 us
    all_to_all x1 -> x2, blocking collectives: 28.6 us -> 80.1 us  [scan_states(): groups = lax.all_to_all(total, 'wide', 0, 0, tiled=True)]
    all_to_all x1 -> x0, waiting for transfers between devices: 26 us -> none  [scan_states(): groups = lax.all_to_all(total, 'wide', 0, 0, tiled=True)]
    all_to_all x1 -> x0, starting transfers between devices: 25.6 us -> none  [scan_states(): groups = lax.all_to_all(total, 'wide', 0, 0, tiled=True)]
    unnamed x18 -> x10, local copies, waits for them, and re-layouts: 3.23 us -> 0.02 us
  transfers between devices with their start and end apart: 3 -> 2, of which waited for: 3 -> 2; matrix products, arithmetic and copies ran while one was open for 0% -> 0% of each run, Pallas kernels for 1% -> 1%
where the time goes in v3:
time: 156 us; the launch traced here: 155 us
  blocking collectives  119 us (76%)
  waiting for transfers between devices  16.5 us (11%)
  Pallas kernels  11.2 us (7%)
  starting transfers between devices  7.64 us (5%)
    all_to_all x2, blocking collectives, scan_states(): groups = lax.all_to_all(total, 'wide', 0, 0, tiled=True)  80.1 us
    all_to_all x2, blocking collectives, scan_states(): pieces = lax.all_to_all(pieces, 'near', 0, 0, tiled=True)  30.5 us
    all_to_all x2, waiting for transfers between devices, scan_states(): return lax.all_to_all(states, 'near', 0, 0, tiled=True)  16.5 us
    pallas_call x10, Pallas kernels, on_chip(): pl.pallas_call(kernel, out_shape=outs, in_specs=specs, out_specs=[pl.Bloc...  11.2 us
    all_to_all x1, blocking collectives, local(): sums = lax.all_to_all(sums, 'fsdp', 0, 0, tiled=True)  8.53 us
    all_to_all x2, starting transfers between devices, scan_states(): return lax.all_to_all(states, 'near', 0, 0, tiled=True)  7.64 us
  transfers between devices with their start and end apart: 2, of which 2 were waited for; matrix products, arithmetic and copies ran while one was open for 0% of the time, Pallas kernels for 1%

profile of v3, /device:TPU:2, one launch (start us, length us, event | category | flops | bytes accessed | tf_op | source)
XLA Modules:
  0.0 155.2 jit_solution(13591680157200732197)
XLA Ops:
  0.6 2.2 %summary.1 = (f32[16,24,128]{2,1,0:T(8,128)S(1)}, f32[8,256]{1,0:T(8,128)S(1)}, f32[256,16]{1,0:T(8,128)S(1)}) custom-call(s32[256]{0:T(256)} %segment_ref.1, f32[4,256]{1,0:T(4,128)} %decay_ref.1, bf16[256,384]{1,0:T(8,128)(2,1)} %key_ref.7, bf16[256,384]{1,0:T(8,128)(2,1)} %value_ref.7), custom_call_target="tpu_custom_call" | custom-call | flops 50331648 | bytes 398336 | tf_op jit(solution)/shard_map/summary/pallas_call | solution.py:32
  2.8 18.1 %all_to_all.35.pieces_ref = f32[16,24,128]{2,1,0:T(8,128)S(1)} all-to-all(f32[16,24,128]{2,1,0:T(8,128)S(1)} %get-tuple-element.25), channel_id=1, replica_groups=mesh['wide'=8,'near'=16,'fsdp'=8] {'near'}, dimensions={0} | all-to-all | bytes 393216 | tf_op jit(solution)/shard_map/all_to_all | solution.py:258
  20.9 0.3 group_total.2
  21.2 51.5 %all_to_all.36.groups_ref = f32[8,24,128]{2,1,0:T(8,128)S(1)} all-to-all(f32[8,24,128]{2,1,0:T(8,128)S(1)} %group_total.2), channel_id=1, replica_groups=mesh['wide'=8,'near'=16,'fsdp'=8] {'wide'}, dimensions={0} | all-to-all | bytes 196608 | tf_op jit(solution)/shard_map/all_to_all | solution.py:266
  72.7 1.5 group_prefix.2
  74.2 4.1 %all-to-all-start.2 = ((f32[16,24,128]{2,1,0:T(8,128)}), f32[16,24,128]{2,1,0:T(8,128)S(1)}, u32[]{:S(2)}, u32[]{:S(2)}) async-start(f32[16,24,128]{2,1,0:T(8,128)} %group_prefix.2), calls=%async_computation.2 | async-start | bytes 393216 | tf_op jit(solution)/shard_map/all_to_all | solution.py:273
  78.3 0.0 copy-done.4
  78.4 0.0 copy-done.2
  78.4 0.0 copy-done
  78.4 0.0 copy-done.1
  78.4 0.0 copy-start.3
  78.4 0.6 inside.1
  79.0 8.8 %all-to-all-done.2.states_ref = f32[16,24,128]{2,1,0:T(8,128)S(1)} async-done(((f32[16,24,128]{2,1,0:T(8,128)}), f32[16,24,128]{2,1,0:T(8,128)S(1)}, u32[]{:S(2)}, u32[]{:S(2)}) %all-to-all-start.2) | async-done | bytes 196640 | tf_op jit(solution)/shard_map/all_to_all | solution.py:273
  87.8 0.6 attention.1
  88.4 8.5 %all_to_all.37.sums_ref = f32[8,2,256]{2,1,0:T(2,128)S(1)} all-to-all(f32[8,2,256]{2,1,0:T(2,128)S(1)} %get-tuple-element.27), channel_id=1, replica_groups=mesh['wide'=8,'near'=16,'fsdp'=8] {'fsdp'}, dimensions={0} | all-to-all | bytes 32768 | tf_op jit(solution)/shard_map/all_to_all | solution.py:312
  97.0 1.0 gradient.1
  98.0 12.5 %all_to_all.38.pieces_ref = f32[16,24,128]{2,1,0:T(8,128)S(1)} all-to-all(f32[16,24,128]{2,1,0:T(8,128)S(1)} %get-tuple-element.33), channel_id=1, replica_groups=mesh['wide'=8,'near'=16,'fsdp'=8] {'near'}, dimensions={0} | all-to-all | bytes 393216 | tf_op jit(solution)/shard_map/all_to_all | solution.py:258
  110.4 0.3 group_total.3
  110.7 28.6 %all_to_all.39.groups_ref = f32[8,24,128]{2,1,0:T(8,128)S(1)} all-to-all(f32[8,24,128]{2,1,0:T(8,128)S(1)} %group_total.3), channel_id=1, replica_groups=mesh['wide'=8,'near'=16,'fsdp'=8] {'wide'}, dimensions={0} | all-to-all | bytes 196608 | tf_op jit(solution)/shard_map/all_to_all | solution.py:266
  139.3 1.5 group_prefix.3
  140.9 3.5 %all-to-all-start.6 = ((f32[16,24,128]{2,1,0:T(8,128)}), f32[16,24,128]{2,1,0:T(8,128)S(1)}, u32[]{:S(2)}, u32[]{:S(2)}) async-start(f32[16,24,128]{2,1,0:T(8,128)} %group_prefix.3), calls=%async_computation.6 | async-start | bytes 393216 | tf_op jit(solution)/shard_map/all_to_all | solution.py:273
  144.4 1.8 %inside_back.1 = (bf16[256,384]{1,0:T(8,128)(2,1)}, f32[256,384]{1,0:T(8,128)S(1)}, f32[256,384]{1,0:T(8,128)S(1)}, bf16[256,384]{1,0:T(8,128)(2,1)}) custom-call(f32[8,256]{1,0:T(8,128)S(1)} %get-tuple-element.22.rows_ref, f32[256,16]{1,0:T(8,128)S(1)} %get-tuple-element.23.cols_ref, bf16[256,384]{1,0:T(8,128)(2,1)S(1)} %copy-done, ...), custom_call_target="tpu_custom_call" | custom-call | flops 402653184 | bytes 2328064 | tf_op jit(solution)/shard_map/inside_back/pallas_call | solution.py:32
  146.2 7.6 %all-to-all-done.6.states_ref = f32[16,24,128]{2,1,0:T(8,128)S(1)} async-done(((f32[16,24,128]{2,1,0:T(8,128)}), f32[16,24,128]{2,1,0:T(8,128)S(1)}, u32[]{:S(2)}, u32[]{:S(2)}) %all-to-all-start.6) | async-done | bytes 196640 | tf_op jit(solution)/shard_map/all_to_all | solution.py:273
  153.8 1.4 last.1
  (6 shorter events, 0.0 us)
Async XLA Ops:
  72.7 5.7 %copy-start.4 = (f32[384]{0:T(512)S(1)}, f32[384]{0:T(512)}, u32[]{:S(2)}) copy-start(f32[384]{0:T(512)} %param.12) | copy-start | bytes 4612
  72.7 5.7 %copy-start.2 = (bf16[256,384]{1,0:T(8,128)(2,1)S(1)}, bf16[256,384]{1,0:T(8,128)(2,1)}, u32[]{:S(2)}) copy-start(bf16[256,384]{1,0:T(8,128)(2,1)} %value_ref.7) | copy-start | bytes 589828
  74.2 4.2 %copy-start = (bf16[256,384]{1,0:T(8,128)(2,1)S(1)}, bf16[256,384]{1,0:T(8,128)(2,1)}, u32[]{:S(2)}) copy-start(bf16[256,384]{1,0:T(8,128)(2,1)} %query_ref.7) | copy-start | bytes 589828
  74.2 4.2 %copy-start.1 = (bf16[256,384]{1,0:T(8,128)(2,1)S(1)}, bf16[256,384]{1,0:T(8,128)(2,1)}, u32[]{:S(2)}) copy-start(bf16[256,384]{1,0:T(8,128)(2,1)} %key_ref.7) | copy-start | bytes 589828
  74.2 13.6 %all-to-all-start.2 = ((f32[16,24,128]{2,1,0:T(8,128)}), f32[16,24,128]{2,1,0:T(8,128)S(1)}, u32[]{:S(2)}, u32[]{:S(2)}) async-start(f32[16,24,128]{2,1,0:T(8,128)} %group_prefix.2), calls=%async_computation.2 | async-start | bytes 393216 | tf_op jit(solution)/shard_map/all_to_all | solution.py:273
  78.4 9.4 %copy-start.3 = (bf16[256,384]{1,0:T(8,128)(2,1)S(1)}, bf16[256,384]{1,0:T(8,128)(2,1)}, u32[]{:S(2)}) copy-start(bf16[256,384]{1,0:T(8,128)(2,1)} %grad_ref.3) | copy-start | bytes 589828
  140.9 12.9 %all-to-all-start.6 = ((f32[16,24,128]{2,1,0:T(8,128)}), f32[16,24,128]{2,1,0:T(8,128)S(1)}, u32[]{:S(2)}, u32[]{:S(2)}) async-start(f32[16,24,128]{2,1,0:T(8,128)} %group_prefix.3), calls=%async_computation.6 | async-start | bytes 393216 | tf_op jit(solution)/shard_map/all_to_all | solution.py:273

commit v4 on v3

--- a/solution.py
+++ b/solution.py
@@ -46,6 +46,10 @@
     return lax.dot_general(
         a, b, (((over_a,), (over_b,)), ((), ())), preferred_element_type=jnp.float32
     )
+
+
+def row_of(ref):
+    return ref[...].reshape(1, ref.shape[0])
 
 
 def pick_heads(parts, tile, rows):
@@ -163,7 +167,7 @@
     return jnp.concatenate(tiles, axis=1)
 
 
-def inside_kernel(rows_ref, cols_ref, query_ref, key_ref, value_ref, probs_ref, inner_ref):
+def inside_kernel(rows_ref, cols_ref, query_ref, key_ref, value_ref, probs_ref, inner_ref, ready_ref):
     query, key = query_ref[...], key_ref[...]
     weights = []
     for h, mask in decay_masks(rows_ref, cols_ref):
@@ -172,6 +176,7 @@
         weights.append((scores * mask).astype(jnp.bfloat16))
         probs_ref[h] = weights[h]
     inner_ref[...] = times_heads(weights, value_ref[...], 1)
+    ready_ref[...] = jnp.zeros(ready_ref.shape, jnp.float32)
 
 
 def attention_kernel(
@@ -183,7 +188,7 @@
     attention = inner_ref[...] + outer * over_features(cols_ref[...], 0, BLOCK)
     attention_ref[...] = attention
     squares = attention * attention
-    products = grad_ref[...].astype(jnp.float32) * gain_ref[...] * attention
+    products = grad_ref[...].astype(jnp.float32) * row_of(gain_ref) * attention
     sums = []
     for x in (squares, products):
         x = x[:, :TILE] + x[:, TILE : 2 * TILE] + x[:, 2 * TILE :]
@@ -208,7 +213,7 @@
     inv, dots = both[:, 0:1], both[:, 1:2]
     normed = attention_ref[...] * inv
     grad = grad_ref[...].astype(jnp.float32)
-    grad_attn = (inv * (grad * gain_ref[...] - normed * dots)).astype(jnp.bfloat16)
+    grad_attn = (inv * (grad * row_of(gain_ref) - normed * dots)).astype(jnp.bfloat16)
     grad_attn_ref[...] = grad_attn
     gain = jnp.sum(grad * normed, axis=0, keepdims=True)
     gain = jnp.transpose(jnp.broadcast_to(gain, (8, gain.shape[1])))
@@ -219,7 +224,7 @@
 def inside_back_kernel(
     rows_ref, cols_ref, query_ref, key_ref, value_ref, probs_ref, grad_attn_ref, states_ref,
     attention_ref, inv_ref, gain_ref,
-    grad_query_ref, part_key_ref, part_value_ref, attended_ref,
+    grad_query_ref, part_key_ref, part_value_ref, attended_ref, ready_ref,
 ):
     grad_attn, value = grad_attn_ref[...], value_ref[...]
     weights = []
@@ -233,8 +238,9 @@
     grad_query_ref[...] = grad_query.astype(jnp.bfloat16)
     part_key_ref[...] = times_heads(weights, query_ref[...], 0)
     part_value_ref[...] = times_heads([probs_ref[h] for h in range(HEADS)], grad_attn, 0)
-    attended = attention_ref[...] * inv_ref[:, 0:1] * gain_ref[...]
+    attended = attention_ref[...] * inv_ref[:, 0:1] * row_of(gain_ref)
     attended_ref[...] = attended.astype(jnp.bfloat16)
+    ready_ref[...] = jnp.zeros(ready_ref.shape, jnp.float32)
 
 
 def last_kernel(
@@ -253,21 +259,31 @@
     grad_gain_ref[...] = (jnp.transpose(gain)[GAIN : GAIN + 1] * scale).reshape(gain.shape[0])
 
 
-def scan_states(pieces, backward):
+def reach_owners(pieces, backward):
     group, sub, lanes = pieces.shape
     pieces = lax.all_to_all(pieces, "near", 0, 0, tiled=True)
-    group_count = lax.axis_size("wide")
     (total,) = on_chip(
         functools.partial(total_kernel, backward),
-        [pltpu.VMEM((group_count, sub, lanes), jnp.float32)],
+        [pltpu.VMEM((lax.axis_size("wide"), sub, lanes), jnp.float32)],
         [pieces],
         "group_total",
     )
     groups = lax.all_to_all(total, "wide", 0, 0, tiled=True)
+    inside = on_chip(
+        functools.partial(local_prefix_kernel, backward),
+        [pltpu.VMEM(pieces.shape, jnp.float32), pltpu.VMEM(pieces.shape, jnp.float32)],
+        [pieces],
+        "local_prefix",
+        flops=8 * pieces.size,
+    )
+    return (*inside, groups)
+
+
+def leave_owners(local_states, factors, groups, ready, backward):
     (states,) = on_chip(
         functools.partial(prefix_kernel, backward),
-        [pltpu.VMEM((group, sub, lanes), jnp.float32)],
-        [pieces, groups],
+        [pltpu.VMEM(local_states.shape, jnp.float32)],
+        [local_states, factors, groups, ready],
         "group_prefix",
     )
     return lax.all_to_all(states, "near", 0, 0, tiled=True)
@@ -292,20 +308,25 @@
         flops=mxu,
         held_in=pltpu.HBM,
     )
-    probs, inner = on_chip(
+    scan = reach_owners(pieces, False)
+    ready_shape = pltpu.VMEM((8, TILE), jnp.float32)
+    probs, inner, ready = on_chip(
         inside_kernel,
-        [pltpu.VMEM((HEADS, tokens, tokens), jnp.bfloat16), pltpu.VMEM(full, jnp.float32)],
+        [
+            pltpu.VMEM((HEADS, tokens, tokens), jnp.bfloat16),
+            pltpu.VMEM(full, jnp.float32),
+            ready_shape,
+        ],
         [rows, cols, queries, key_rows, values],
         "inside",
         flops=4 * mxu,
         exps=HEADS * tokens * tokens,
     )
-    state_in = scan_states(pieces, False)
-    gain_row = norm_gain.reshape(1, features)
+    state_in = leave_owners(*scan, ready, False)
     attention, sums = on_chip(
         attention_kernel,
         [pltpu.VMEM(full, jnp.float32), pltpu.VMEM((fsdp, 2, tokens), jnp.float32)],
-        [state_in, inner, cols, queries, grad_out, gain_row],
+        [state_in, inner, cols, queries, grad_out, norm_gain],
         "attention",
         flops=2 * mxu,
     )
@@ -317,24 +338,26 @@
             pltpu.VMEM((tokens, 8), jnp.float32),
             pltpu.VMEM((group, SUB, TILE), jnp.float32),
         ],
-        [sums, attention, grad_out, gain_row, rows, cols, queries],
+        [sums, attention, grad_out, norm_gain, rows, cols, queries],
         "gradient",
         flops=mxu,
     )
-    grad_queries, part_key, part_value, attended = on_chip(
+    back_scan = reach_owners(back_pieces, True)
+    grad_queries, part_key, part_value, attended, back_ready = on_chip(
         inside_back_kernel,
         [
             jax.ShapeDtypeStruct(full, jnp.bfloat16),
             pltpu.VMEM(full, jnp.float32),
             pltpu.VMEM(full, jnp.float32),
             jax.ShapeDtypeStruct(full, jnp.bfloat16),
+            ready_shape,
         ],
-        [rows, cols, queries, key_rows, values, probs, grad_attn, state_in, attention, inv, gain_row],
+        [rows, cols, queries, key_rows, values, probs, grad_attn, state_in, attention, inv, norm_gain],
         "inside_back",
         flops=8 * mxu,
         exps=HEADS * tokens * tokens,
     )
-    back_in = scan_states(back_pieces, True)
+    back_in = leave_owners(*back_scan, back_ready, True)
     grad_keys, grad_values, grad_gain = on_chip(
         functools.partial(last_kernel, float(tokens * dp_count) ** (-0.5)),
         [
@@ -379,38 +402,46 @@
         out_ref[g] = out
 
 
-def prefix_kernel(backward, pieces_ref, groups_ref, out_ref):
+def local_prefix_kernel(backward, pieces_ref, local_ref, factor_ref):
     count, rows, lanes = pieces_ref.shape
-    group_count = groups_ref.shape[0]
-    mine = lax.axis_index("wide")
-    lane = lax.broadcasted_iota(jnp.int32, (rows, lanes), 1)
-    group_order = list(range(group_count))[::-1] if backward else list(range(group_count))
-    running = jnp.zeros((rows, lanes), jnp.float32)
-    gain = jnp.zeros((rows, lanes), jnp.float32)
-    last_far = jnp.full((rows, 1), -1.0, jnp.float32)
-    entering = running
-    entering_far = last_far
-    for g in group_order:
-        here = mine == g
-        entering = jnp.where(here, running, entering)
-        entering_far = jnp.where(here, last_far, entering_far)
-        piece = groups_ref[g]
-        joined = (last_far == piece[:, NEAR : NEAR + 1]).astype(jnp.float32)
-        running = piece + (piece[:, PASS : PASS + 1] * joined) * running
-        gain = gain + piece
-        last_far = piece[:, FAR : FAR + 1]
     order = list(range(count))[::-1] if backward else list(range(count))
     passes, near, far = columns(pieces_ref, count)
     if backward:
         near, far = far, near
-    state = entering
-    before_far = entering_far
-    for k in order:
-        joined = (before_far == near[k]).astype(jnp.float32)
-        state = state * joined
-        out_ref[k] = jnp.where(lane < PASS, state, gain)
-        state = pieces_ref[k] + passes[k] * state
-        before_far = far[k]
+    state = jnp.zeros((rows, lanes), jnp.float32)
+    factor = jnp.ones((rows, lanes), jnp.float32)
+    local_ref[order[0]] = state
+    factor_ref[order[0]] = factor
+    for before, k in zip(order[:-1], order[1:]):
+        joined = (far[before] == near[k]).astype(jnp.float32)
+        carried = jnp.broadcast_to(passes[before] * joined, (rows, lanes))
+        state = pieces_ref[before] * joined + carried * state
+        factor = carried * factor
+        local_ref[k] = state
+        factor_ref[k] = factor
+
+
+def prefix_kernel(backward, local_ref, factor_ref, groups_ref, ready_ref, out_ref):
+    del ready_ref
+    count, rows, lanes = local_ref.shape
+    group_count = groups_ref.shape[0]
+    mine = lax.axis_index("wide")
+    lane = lax.broadcasted_iota(jnp.int32, (rows, lanes), 1)
+    running = jnp.zeros((rows, lanes), jnp.float32)
+    gain = jnp.zeros((rows, lanes), jnp.float32)
+    entering = running
+    order = list(range(group_count))[::-1] if backward else list(range(group_count))
+    passes, near, far = columns(groups_ref, group_count)
+    for at, g in enumerate(order):
+        if at:
+            running = running * (far[order[at - 1]] == near[g]).astype(jnp.float32)
+        entering = jnp.where(mine == g, running, entering)
+        piece = groups_ref[g]
+        running = piece + passes[g] * running
+        gain = gain + piece
+    states = [jnp.where(lane < PASS, local_ref[k] + factor_ref[k] * entering, gain) for k in range(count)]
+    for k in range(count):
+        out_ref[k] = states[k]
 
 
 def solution(mesh):

time: 156 us -> 155 us (level)
  blocking collectives: 119 us -> 65.3 us
  waiting for transfers between devices: 16.5 us -> 49 us
  starting transfers between devices: 7.64 us -> 29 us
    all_to_all x4, blocking collectives: 111 us -> 56.8 us  [the longest x2 30.7 us: reach_owners(): pieces = lax.all_to_all(pieces, 'near', 0, 0, tiled=True)]
    all_to_all x2, waiting for transfers between devices: 16.5 us -> 49 us  [reach_owners(): groups = lax.all_to_all(total, 'wide', 0, 0, tiled=True)]
    all_to_all x2, starting transfers between devices: 7.64 us -> 29 us  [reach_owners(): groups = lax.all_to_all(total, 'wide', 0, 0, tiled=True)]
    pallas_call x10 -> x12, Pallas kernels: 11.2 us -> 10.6 us  [on_chip(): pl.pallas_call(kernel, out_shape=outs, in_specs=specs, out_specs=[pl.Bloc...]
  transfers between devices with their start and end apart: 2 -> 2, of which waited for: 2 -> 2; matrix products, arithmetic and copies ran while one was open for 0% -> 0% of each run, Pallas kernels for 1% -> 2%
where the time goes in v4:
time: 155 us
  blocking collectives  65.3 us (42%)
  waiting for transfers between devices  49 us (32%)
  starting transfers between devices  29 us (19%)
  Pallas kernels  10.6 us (7%)
    all_to_all x2, waiting for transfers between devices, reach_owners(): groups = lax.all_to_all(total, 'wide', 0, 0, tiled=True)  49 us
    all_to_all x2, blocking collectives, reach_owners(): pieces = lax.all_to_all(pieces, 'near', 0, 0, tiled=True)  30.7 us
    all_to_all x2, starting transfers between devices, reach_owners(): groups = lax.all_to_all(total, 'wide', 0, 0, tiled=True)  29 us
    all_to_all x2, blocking collectives, leave_owners(): return lax.all_to_all(states, 'near', 0, 0, tiled=True)  26.2 us
    pallas_call x12, Pallas kernels, on_chip(): pl.pallas_call(kernel, out_shape=outs, in_specs=specs, out_specs=[pl.Bloc...  10.6 us
    all_to_all x1, blocking collectives, local(): sums = lax.all_to_all(sums, 'fsdp', 0, 0, tiled=True)  8.53 us
  transfers between devices with their start and end apart: 2, of which 2 were waited for; matrix products, arithmetic and copies ran while one was open for 0% of the time, Pallas kernels for 2%

profile of v4, /device:TPU:2, one launch (start us, length us, event | category | flops | bytes accessed | tf_op | source)
XLA Modules:
  0.0 154.8 jit_solution(14901927721553529021)
XLA Ops:
  0.6 2.2 %summary.1 = (f32[16,24,128]{2,1,0:T(8,128)S(1)}, f32[8,256]{1,0:T(8,128)S(1)}, f32[256,16]{1,0:T(8,128)S(1)}) custom-call(s32[256]{0:T(256)} %segment_ref.1, f32[4,256]{1,0:T(4,128)} %decay_ref.1, bf16[256,384]{1,0:T(8,128)(2,1)} %key_ref.7, bf16[256,384]{1,0:T(8,128)(2,1)} %value_ref.7), custom_call_target="tpu_custom_call" | custom-call | flops 50331648 | bytes 398336 | tf_op jit(solution)/shard_map/summary/pallas_call | solution.py:32
  2.8 0.0 copy-start.2
  2.9 18.2 %all_to_all.35.pieces_ref = f32[16,24,128]{2,1,0:T(8,128)S(1)} all-to-all(f32[16,24,128]{2,1,0:T(8,128)S(1)} %get-tuple-element.31), channel_id=1, replica_groups=mesh['wide'=8,'near'=16,'fsdp'=8] {'near'}, dimensions={0} | all-to-all | bytes 393216 | tf_op jit(solution)/shard_map/all_to_all | solution.py:264
  21.1 0.9 group_total.2
  22.0 25.6 %all-to-all-start.1 = ((f32[8,24,128]{2,1,0:T(8,128)}), f32[8,24,128]{2,1,0:T(8,128)S(1)}, u32[]{:S(2)}, u32[]{:S(2)}) async-start(f32[8,24,128]{2,1,0:T(8,128)} %group_total.2), calls=%async_computation.1 | async-start | bytes 196608 | tf_op jit(solution)/shard_map/all_to_all | solution.py:271
  47.6 0.6 inside.1
  48.2 0.4 local_prefix.2
  48.6 25.0 %all-to-all-done.1.groups_ref = f32[8,24,128]{2,1,0:T(8,128)S(1)} async-done(((f32[8,24,128]{2,1,0:T(8,128)}), f32[8,24,128]{2,1,0:T(8,128)S(1)}, u32[]{:S(2)}, u32[]{:S(2)}) %all-to-all-start.1) | async-done | bytes 98336 | tf_op jit(solution)/shard_map/all_to_all | solution.py:271
  73.7 0.2 group_prefix.2
  73.9 0.0 copy-start.3
  73.9 0.0 copy-start.4
  73.9 13.4 %all_to_all.36.states_ref = f32[16,24,128]{2,1,0:T(8,128)S(1)} all-to-all(f32[16,24,128]{2,1,0:T(8,128)S(1)} %group_prefix.2), channel_id=1, replica_groups=mesh['wide'=8,'near'=16,'fsdp'=8] {'near'}, dimensions={0} | all-to-all | bytes 393216 | tf_op jit(solution)/shard_map/all_to_all | solution.py:289
  87.3 0.6 attention.1
  87.9 8.5 %all_to_all.37.sums_ref = f32[8,2,256]{2,1,0:T(2,128)S(1)} all-to-all(f32[8,2,256]{2,1,0:T(2,128)S(1)} %get-tuple-element.36), channel_id=1, replica_groups=mesh['wide'=8,'near'=16,'fsdp'=8] {'fsdp'}, dimensions={0} | all-to-all | bytes 32768 | tf_op jit(solution)/shard_map/all_to_all | solution.py:333
  96.4 1.0 gradient.1
  97.4 12.5 %all_to_all.38.pieces_ref = f32[16,24,128]{2,1,0:T(8,128)S(1)} all-to-all(f32[16,24,128]{2,1,0:T(8,128)S(1)} %get-tuple-element.42), channel_id=1, replica_groups=mesh['wide'=8,'near'=16,'fsdp'=8] {'near'}, dimensions={0} | all-to-all | bytes 393216 | tf_op jit(solution)/shard_map/all_to_all | solution.py:264
  109.9 0.9 group_total.3
  110.8 3.4 %all-to-all-start.5 = ((f32[8,24,128]{2,1,0:T(8,128)}), f32[8,24,128]{2,1,0:T(8,128)S(1)}, u32[]{:S(2)}, u32[]{:S(2)}) async-start(f32[8,24,128]{2,1,0:T(8,128)} %group_total.3), calls=%async_computation.5 | async-start | bytes 196608 | tf_op jit(solution)/shard_map/all_to_all | solution.py:271
  114.2 1.8 %inside_back.1 = (bf16[256,384]{1,0:T(8,128)(2,1)}, f32[256,384]{1,0:T(8,128)S(1)}, f32[256,384]{1,0:T(8,128)S(1)}, bf16[256,384]{1,0:T(8,128)(2,1)}, f32[8,128]{1,0:T(8,128)S(1)}) custom-call(f32[8,256]{1,0:T(8,128)S(1)} %get-tuple-element.28.rows_ref, f32[256,16]{1,0:T(8,128)S(1)} %get-tuple-element.29.cols_ref, bf16[256,384]{1,0:T(8,128)(2,1)S(1)} %copy-done, ...), custom_call_target="tpu_custom_call" | custom-call | flops 402653184 | bytes 2328064 | tf_op jit(solution)/shard_map/inside_back/pallas_call | solution.py:32
  115.9 0.4 local_prefix.3
  116.4 24.0 %all-to-all-done.5.groups_ref = f32[8,24,128]{2,1,0:T(8,128)S(1)} async-done(((f32[8,24,128]{2,1,0:T(8,128)}), f32[8,24,128]{2,1,0:T(8,128)S(1)}, u32[]{:S(2)}, u32[]{:S(2)}) %all-to-all-start.5) | async-done | bytes 98336 | tf_op jit(solution)/shard_map/all_to_all | solution.py:271
  140.4 0.2 group_prefix.3
  140.6 12.8 %all_to_all.39.states_ref = f32[16,24,128]{2,1,0:T(8,128)S(1)} all-to-all(f32[16,24,128]{2,1,0:T(8,128)S(1)} %group_prefix.3), channel_id=1, replica_groups=mesh['wide'=8,'near'=16,'fsdp'=8] {'near'}, dimensions={0} | all-to-all | bytes 393216 | tf_op jit(solution)/shard_map/all_to_all | solution.py:289
  153.4 1.4 last.1
  (7 shorter events, 0.0 us)
Async XLA Ops:
  2.8 44.8 %copy-start.2 = (bf16[256,384]{1,0:T(8,128)(2,1)S(1)}, bf16[256,384]{1,0:T(8,128)(2,1)}, u32[]{:S(2)}) copy-start(bf16[256,384]{1,0:T(8,128)(2,1)} %value_ref.7) | copy-start | bytes 589828
  21.1 26.6 %copy-start = (bf16[256,384]{1,0:T(8,128)(2,1)S(1)}, bf16[256,384]{1,0:T(8,128)(2,1)}, u32[]{:S(2)}) copy-start(bf16[256,384]{1,0:T(8,128)(2,1)} %query_ref.7) | copy-start | bytes 589828
  21.1 26.6 %copy-start.1 = (bf16[256,384]{1,0:T(8,128)(2,1)S(1)}, bf16[256,384]{1,0:T(8,128)(2,1)}, u32[]{:S(2)}) copy-start(bf16[256,384]{1,0:T(8,128)(2,1)} %key_ref.7) | copy-start | bytes 589828
  22.0 51.7 %all-to-all-start.1 = ((f32[8,24,128]{2,1,0:T(8,128)}), f32[8,24,128]{2,1,0:T(8,128)S(1)}, u32[]{:S(2)}, u32[]{:S(2)}) async-start(f32[8,24,128]{2,1,0:T(8,128)} %group_total.2), calls=%async_computation.1 | async-start | bytes 196608 | tf_op jit(solution)/shard_map/all_to_all | solution.py:271
  73.9 13.4 %copy-start.3 = (bf16[256,384]{1,0:T(8,128)(2,1)S(1)}, bf16[256,384]{1,0:T(8,128)(2,1)}, u32[]{:S(2)}) copy-start(bf16[256,384]{1,0:T(8,128)(2,1)} %grad_ref.3) | copy-start | bytes 589828
  73.9 13.4 %copy-start.4 = (f32[384]{0:T(512)S(1)}, f32[384]{0:T(512)}, u32[]{:S(2)}) copy-start(f32[384]{0:T(512)} %gain_ref.5) | copy-start | bytes 4612
  110.8 29.6 %all-to-all-start.5 = ((f32[8,24,128]{2,1,0:T(8,128)}), f32[8,24,128]{2,1,0:T(8,128)S(1)}, u32[]{:S(2)}, u32[]{:S(2)}) async-start(f32[8,24,128]{2,1,0:T(8,128)} %group_total.3), calls=%async_computation.5 | async-start | bytes 196608 | tf_op jit(solution)/shard_map/all_to_all | solution.py:271

commit v5 on v4

--- a/solution.py
+++ b/solution.py
@@ -16,8 +16,19 @@
 
 HEADS, HEAD, TILE = 4, 96, 128
 SUB = 24
+NEAR_ORDER = (5, 1, 2, 3, 4, 0, 6, 7, 8, 9, 10, 11, 12, 13, 14, 15)
+WIDE_ORDER = (4, 5, 6, 7, 0, 1, 2, 3)
 STARTS = tuple(HEAD * h % TILE for h in range(HEADS))
 WINDOWS = tuple((HEAD * h // TILE, (HEAD * h + HEAD - 1) // TILE + 1) for h in range(HEADS))
+
+
+def exchange(x, axis, order):
+    return lax.all_to_all(x, axis, 0, 0, axis_index_groups=[list(order)], tiled=True)
+
+
+def places(order, backward):
+    found = [order.index(k) for k in range(len(order))]
+    return found[::-1] if backward else found
 
 
 def on_chip(kernel, outs, operands, name, flops=0, exps=0, held_in=pltpu.VMEM):
@@ -261,14 +272,14 @@
 
 def reach_owners(pieces, backward):
     group, sub, lanes = pieces.shape
-    pieces = lax.all_to_all(pieces, "near", 0, 0, tiled=True)
+    pieces = exchange(pieces, "near", NEAR_ORDER)
     (total,) = on_chip(
         functools.partial(total_kernel, backward),
         [pltpu.VMEM((lax.axis_size("wide"), sub, lanes), jnp.float32)],
         [pieces],
         "group_total",
     )
-    groups = lax.all_to_all(total, "wide", 0, 0, tiled=True)
+    groups = exchange(total, "wide", WIDE_ORDER)
     inside = on_chip(
         functools.partial(local_prefix_kernel, backward),
         [pltpu.VMEM(pieces.shape, jnp.float32), pltpu.VMEM(pieces.shape, jnp.float32)],
@@ -286,7 +297,7 @@
         [local_states, factors, groups, ready],
         "group_prefix",
     )
-    return lax.all_to_all(states, "near", 0, 0, tiled=True)
+    return exchange(states, "near", NEAR_ORDER)
 
 
 def local(queries, key_rows, values, log_decay, segment_ids, norm_gain, grad_out):
@@ -379,7 +390,7 @@
 
 def total_kernel(backward, pieces_ref, out_ref):
     count, rows, lanes = pieces_ref.shape
-    order = list(range(count))[::-1] if backward else list(range(count))
+    order = places(NEAR_ORDER, backward)
     passes, near, far = columns(pieces_ref, count)
     if backward:
         near, far = far, near
@@ -404,7 +415,7 @@
 
 def local_prefix_kernel(backward, pieces_ref, local_ref, factor_ref):
     count, rows, lanes = pieces_ref.shape
-    order = list(range(count))[::-1] if backward else list(range(count))
+    order = places(NEAR_ORDER, backward)
     passes, near, far = columns(pieces_ref, count)
     if backward:
         near, far = far, near
@@ -430,12 +441,12 @@
     running = jnp.zeros((rows, lanes), jnp.float32)
     gain = jnp.zeros((rows, lanes), jnp.float32)
     entering = running
-    order = list(range(group_count))[::-1] if backward else list(range(group_count))
+    order = places(WIDE_ORDER, backward)
     passes, near, far = columns(groups_ref, group_count)
     for at, g in enumerate(order):
         if at:
             running = running * (far[order[at - 1]] == near[g]).astype(jnp.float32)
-        entering = jnp.where(mine == g, running, entering)
+        entering = jnp.where(mine == WIDE_ORDER[g], running, entering)
         piece = groups_ref[g]
         running = piece + passes[g] * running
         gain = gain + piece

time: 155 us -> 139 us (0.90)
  the two profiles are of different devices: /device:TPU:2 before, /device:TPU:8 now
where the time goes in v5:
time: 139 us
  blocking collectives  73.2 us (53%)
  starting transfers between devices  45.9 us (33%)
  Pallas kernels  10.6 us (8%)
  waiting for transfers between devices  8.11 us (6%)
    all_to_all x4, blocking collectives, exchange(): lax.all_to_all(x, axis, 0, 0, axis_index_groups=[list(order)], tiled=True)  63.7 us
    all_to_all x2, starting transfers between devices, exchange(): lax.all_to_all(x, axis, 0, 0, axis_index_groups=[list(order)], tiled=True)  45.9 us
    pallas_call x12, Pallas kernels, on_chip(): pl.pallas_call(kernel, out_shape=outs, in_specs=specs, out_specs=[pl.Bloc...  10.6 us
    all_to_all x1, blocking collectives, local(): sums = lax.all_to_all(sums, 'fsdp', 0, 0, tiled=True)  9.46 us
    all_to_all x2, waiting for transfers between devices, exchange(): lax.all_to_all(x, axis, 0, 0, axis_index_groups=[list(order)], tiled=True)  8.11 us
  transfers between devices with their start and end apart: 2, of which 2 were waited for; matrix products, arithmetic and copies ran while one was open for 0% of the time, Pallas kernels for 2%

profile of v5, /device:TPU:8, one launch (start us, length us, event | category | flops | bytes accessed | tf_op | source)
XLA Modules:
  0.0 138.6 jit_solution(18217405716087770733)
XLA Ops:
  0.6 2.2 %summary.1 = (f32[16,24,128]{2,1,0:T(8,128)S(1)}, f32[8,256]{1,0:T(8,128)S(1)}, f32[256,16]{1,0:T(8,128)S(1)}) custom-call(s32[256]{0:T(256)} %segment_ref.1, f32[4,256]{1,0:T(4,128)} %decay_ref.1, bf16[256,384]{1,0:T(8,128)(2,1)} %key_ref.7, bf16[256,384]{1,0:T(8,128)(2,1)} %value_ref.7), custom_call_target="tpu_custom_call" | custom-call | flops 50331648 | bytes 398336 | tf_op jit(solution)/shard_map/summary/pallas_call | solution.py:43
  2.8 0.0 copy-start.2
  2.9 23.9 %all_to_all.35.pieces_ref = f32[16,24,128]{2,1,0:T(8,128)S(1)} all-to-all(f32[16,24,128]{2,1,0:T(8,128)S(1)} %get-tuple-element.31), channel_id=1, replica_groups={{40,8,16,24,32,0,48,56,64,72,80,88,96,104,112,120},{41,9,17,25,33,1,49,..., dimensions={0} | all-to-all | bytes 393216 | tf_op jit(solution)/shard_map/all_to_all | solution.py:26
  26.7 0.9 group_total.2
  27.6 24.2 %all-to-all-start.1 = ((f32[8,24,128]{2,1,0:T(8,128)}), f32[8,24,128]{2,1,0:T(8,128)S(1)}, u32[]{:S(2)}, u32[]{:S(2)}) async-start(f32[8,24,128]{2,1,0:T(8,128)} %group_total.2), calls=%async_computation.1 | async-start | bytes 196608 | tf_op jit(solution)/shard_map/all_to_all | solution.py:26
  51.9 0.6 inside.1
  52.4 0.4 local_prefix.2
  52.8 4.6 %all-to-all-done.1.groups_ref = f32[8,24,128]{2,1,0:T(8,128)S(1)} async-done(((f32[8,24,128]{2,1,0:T(8,128)}), f32[8,24,128]{2,1,0:T(8,128)S(1)}, u32[]{:S(2)}, u32[]{:S(2)}) %all-to-all-start.1) | async-done | bytes 98336 | tf_op jit(solution)/shard_map/all_to_all | solution.py:26
  57.5 0.2 group_prefix.2
  57.7 0.0 copy-start.3
  57.7 0.0 copy-start.4
  57.7 14.0 %all_to_all.36.states_ref = f32[16,24,128]{2,1,0:T(8,128)S(1)} all-to-all(f32[16,24,128]{2,1,0:T(8,128)S(1)} %group_prefix.2), channel_id=1, replica_groups={{40,8,16,24,32,0,48,56,64,72,80,88,96,104,112,120},{41,9,17,25,33,1,49,..., dimensions={0} | all-to-all | bytes 393216 | tf_op jit(solution)/shard_map/all_to_all | solution.py:26
  71.7 0.6 attention.1
  72.4 9.5 %all_to_all.37.sums_ref = f32[8,2,256]{2,1,0:T(2,128)S(1)} all-to-all(f32[8,2,256]{2,1,0:T(2,128)S(1)} %get-tuple-element.36), channel_id=1, replica_groups=mesh['wide'=8,'near'=16,'fsdp'=8] {'fsdp'}, dimensions={0} | all-to-all | bytes 32768 | tf_op jit(solution)/shard_map/all_to_all | solution.py:344
  81.8 1.0 gradient.1
  82.8 11.7 %all_to_all.38.pieces_ref = f32[16,24,128]{2,1,0:T(8,128)S(1)} all-to-all(f32[16,24,128]{2,1,0:T(8,128)S(1)} %get-tuple-element.42), channel_id=1, replica_groups={{40,8,16,24,32,0,48,56,64,72,80,88,96,104,112,120},{41,9,17,25,33,1,49,..., dimensions={0} | all-to-all | bytes 393216 | tf_op jit(solution)/shard_map/all_to_all | solution.py:26
  94.5 0.9 group_total.3
  95.4 21.7 %all-to-all-start.5 = ((f32[8,24,128]{2,1,0:T(8,128)}), f32[8,24,128]{2,1,0:T(8,128)S(1)}, u32[]{:S(2)}, u32[]{:S(2)}) async-start(f32[8,24,128]{2,1,0:T(8,128)} %group_total.3), calls=%async_computation.5 | async-start | bytes 196608 | tf_op jit(solution)/shard_map/all_to_all | solution.py:26
  117.2 1.8 %inside_back.1 = (bf16[256,384]{1,0:T(8,128)(2,1)}, f32[256,384]{1,0:T(8,128)S(1)}, f32[256,384]{1,0:T(8,128)S(1)}, bf16[256,384]{1,0:T(8,128)(2,1)}, f32[8,128]{1,0:T(8,128)S(1)}) custom-call(f32[8,256]{1,0:T(8,128)S(1)} %get-tuple-element.28.rows_ref, f32[256,16]{1,0:T(8,128)S(1)} %get-tuple-element.29.cols_ref, bf16[256,384]{1,0:T(8,128)(2,1)S(1)} %copy-done, ...), custom_call_target="tpu_custom_call" | custom-call | flops 402653184 | bytes 2328064 | tf_op jit(solution)/shard_map/inside_back/pallas_call | solution.py:43
  118.9 0.4 local_prefix.3
  119.4 3.5 %all-to-all-done.5.groups_ref = f32[8,24,128]{2,1,0:T(8,128)S(1)} async-done(((f32[8,24,128]{2,1,0:T(8,128)}), f32[8,24,128]{2,1,0:T(8,128)S(1)}, u32[]{:S(2)}, u32[]{:S(2)}) %all-to-all-start.5) | async-done | bytes 98336 | tf_op jit(solution)/shard_map/all_to_all | solution.py:26
  122.8 0.2 group_prefix.3
  123.0 14.2 %all_to_all.39.states_ref = f32[16,24,128]{2,1,0:T(8,128)S(1)} all-to-all(f32[16,24,128]{2,1,0:T(8,128)S(1)} %group_prefix.3), channel_id=1, replica_groups={{40,8,16,24,32,0,48,56,64,72,80,88,96,104,112,120},{41,9,17,25,33,1,49,..., dimensions={0} | all-to-all | bytes 393216 | tf_op jit(solution)/shard_map/all_to_all | solution.py:26
  137.2 1.4 %last.1 = (bf16[256,384]{1,0:T(8,128)(2,1)}, bf16[256,384]{1,0:T(8,128)(2,1)}, f32[384]{0:T(512)}) custom-call(f32[16,24,128]{2,1,0:T(8,128)S(1)} %all_to_all.39.states_ref, f32[256,16]{1,0:T(8,128)S(1)} %get-tuple-element.29.cols_ref, bf16[256,384]{1,0:T(8,128)(2,1)S(1)} %copy-done.1, bf16[256,384]{1,0:T(8,128)(2,1)S(1)} %copy-done.2, ...), custom_call_target="tpu_custom_call" | custom-call | flops 201326592 | bytes 1787392 | tf_op jit(solution)/shard_map/last/pallas_call | solution.py:43
  (7 shorter events, 0.0 us)
Async XLA Ops:
  2.8 49.0 %copy-start.2 = (bf16[256,384]{1,0:T(8,128)(2,1)S(1)}, bf16[256,384]{1,0:T(8,128)(2,1)}, u32[]{:S(2)}) copy-start(bf16[256,384]{1,0:T(8,128)(2,1)} %value_ref.7) | copy-start | bytes 589828
  26.7 25.1 %copy-start = (bf16[256,384]{1,0:T(8,128)(2,1)S(1)}, bf16[256,384]{1,0:T(8,128)(2,1)}, u32[]{:S(2)}) copy-start(bf16[256,384]{1,0:T(8,128)(2,1)} %query_ref.7) | copy-start | bytes 589828
  26.7 25.1 %copy-start.1 = (bf16[256,384]{1,0:T(8,128)(2,1)S(1)}, bf16[256,384]{1,0:T(8,128)(2,1)}, u32[]{:S(2)}) copy-start(bf16[256,384]{1,0:T(8,128)(2,1)} %key_ref.7) | copy-start | bytes 589828
  27.6 29.8 %all-to-all-start.1 = ((f32[8,24,128]{2,1,0:T(8,128)}), f32[8,24,128]{2,1,0:T(8,128)S(1)}, u32[]{:S(2)}, u32[]{:S(2)}) async-start(f32[8,24,128]{2,1,0:T(8,128)} %group_total.2), calls=%async_computation.1 | async-start | bytes 196608 | tf_op jit(solution)/shard_map/all_to_all | solution.py:26
  57.7 14.1 %copy-start.3 = (bf16[256,384]{1,0:T(8,128)(2,1)S(1)}, bf16[256,384]{1,0:T(8,128)(2,1)}, u32[]{:S(2)}) copy-start(bf16[256,384]{1,0:T(8,128)(2,1)} %grad_ref.3) | copy-start | bytes 589828
  57.7 14.1 %copy-start.4 = (f32[384]{0:T(512)S(1)}, f32[384]{0:T(512)}, u32[]{:S(2)}) copy-start(f32[384]{0:T(512)} %gain_ref.5) | copy-start | bytes 4612
  95.4 27.4 %all-to-all-start.5 = ((f32[8,24,128]{2,1,0:T(8,128)}), f32[8,24,128]{2,1,0:T(8,128)S(1)}, u32[]{:S(2)}, u32[]{:S(2)}) async-start(f32[8,24,128]{2,1,0:T(8,128)} %group_total.3), calls=%async_computation.5 | async-start | bytes 196608 | tf_op jit(solution)/shard_map/all_to_all | solution.py:26

commit v6 on v5

--- a/solution.py
+++ b/solution.py
@@ -17,7 +17,8 @@
 HEADS, HEAD, TILE = 4, 96, 128
 SUB = 24
 NEAR_ORDER = (5, 1, 2, 3, 4, 0, 6, 7, 8, 9, 10, 11, 12, 13, 14, 15)
-WIDE_ORDER = (4, 5, 6, 7, 0, 1, 2, 3)
+WIDE_ORDER = (5, 6, 7, 0, 1, 2, 3, 4)
+REACH = 4
 STARTS = tuple(HEAD * h % TILE for h in range(HEADS))
 WINDOWS = tuple((HEAD * h // TILE, (HEAD * h + HEAD - 1) // TILE + 1) for h in range(HEADS))
 
@@ -272,14 +273,21 @@
 
 def reach_owners(pieces, backward):
     group, sub, lanes = pieces.shape
+    wide = lax.axis_size("wide")
     pieces = exchange(pieces, "near", NEAR_ORDER)
     (total,) = on_chip(
         functools.partial(total_kernel, backward),
-        [pltpu.VMEM((lax.axis_size("wide"), sub, lanes), jnp.float32)],
+        [pltpu.VMEM((wide, sub, lanes) if backward else (sub, lanes), jnp.float32)],
         [pieces],
         "group_total",
     )
-    groups = exchange(total, "wide", WIDE_ORDER)
+    if backward:
+        groups = [exchange(total, "wide", WIDE_ORDER)]
+    else:
+        groups = [total]
+        for away in range(1, REACH + 1):
+            pairs = [(g, g + away) for g in range(wide - away)]
+            groups.append(lax.ppermute(total, "wide", pairs))
     inside = on_chip(
         functools.partial(local_prefix_kernel, backward),
         [pltpu.VMEM(pieces.shape, jnp.float32), pltpu.VMEM(pieces.shape, jnp.float32)],
@@ -292,9 +300,9 @@
 
 def leave_owners(local_states, factors, groups, ready, backward):
     (states,) = on_chip(
-        functools.partial(prefix_kernel, backward),
+        back_prefix_kernel if backward else prefix_kernel,
         [pltpu.VMEM(local_states.shape, jnp.float32)],
-        [local_states, factors, groups, ready],
+        [local_states, factors, ready, *groups],
         "group_prefix",
     )
     return exchange(states, "near", NEAR_ORDER)
@@ -409,6 +417,9 @@
     out = jnp.where(lane == PASS, through, out)
     out = jnp.where(lane == NEAR, near[first], out)
     out = jnp.where(lane == FAR, far[last], out)
+    if not backward:
+        out_ref[...] = out
+        return
     for g in range(out_ref.shape[0]):
         out_ref[g] = out
 
@@ -432,7 +443,26 @@
         factor_ref[k] = factor
 
 
-def prefix_kernel(backward, local_ref, factor_ref, groups_ref, ready_ref, out_ref):
+def prefix_kernel(local_ref, factor_ref, ready_ref, own_ref, *refs):
+    del ready_ref
+    *group_refs, out_ref = refs
+    count, rows, lanes = local_ref.shape
+    mine = lax.axis_index("wide")
+    running = jnp.zeros((rows, lanes), jnp.float32)
+    before = jnp.full((rows, 1), -1.0, jnp.float32)
+    for away in range(REACH, 0, -1):
+        piece = group_refs[away - 1][...]
+        joined = (before == piece[:, NEAR : NEAR + 1]).astype(jnp.float32)
+        running = piece + (piece[:, PASS : PASS + 1] * joined) * running
+        running = jnp.where(mine >= away, running, 0.0)
+        before = piece[:, FAR : FAR + 1]
+    entering = running * (before == own_ref[:, NEAR : NEAR + 1]).astype(jnp.float32)
+    states = [local_ref[k] + factor_ref[k] * entering for k in range(count)]
+    for k in range(count):
+        out_ref[k] = states[k]
+
+
+def back_prefix_kernel(local_ref, factor_ref, ready_ref, groups_ref, out_ref):
     del ready_ref
     count, rows, lanes = local_ref.shape
     group_count = groups_ref.shape[0]
@@ -441,7 +471,7 @@
     running = jnp.zeros((rows, lanes), jnp.float32)
     gain = jnp.zeros((rows, lanes), jnp.float32)
     entering = running
-    order = places(WIDE_ORDER, backward)
+    order = places(WIDE_ORDER, True)
     passes, near, far = columns(groups_ref, group_count)
     for at, g in enumerate(order):
         if at:

time: 139 us -> 143 us (1.029)
  starting transfers between devices: 45.9 us -> 53.6 us
  blocking collectives: 73.2 us -> 68.8 us
    ppermute x0 -> x4, starting transfers between devices: none -> 31.1 us  [reach_owners(): groups.append(lax.ppermute(total, 'wide', pairs))]
    all_to_all x2 -> x1, starting transfers between devices: 45.9 us -> 22.5 us  [exchange(): lax.all_to_all(x, axis, 0, 0, axis_index_groups=[list(order)], tiled=True)]
    all_to_all x4, blocking collectives: 63.7 us -> 59.3 us  [exchange(): lax.all_to_all(x, axis, 0, 0, axis_index_groups=[list(order)], tiled=True)]
    all_to_all x2 -> x1, waiting for transfers between devices: 8.11 us -> 9.04 us  [exchange(): lax.all_to_all(x, axis, 0, 0, axis_index_groups=[list(order)], tiled=True)]
  transfers between devices with their start and end apart: 2 -> 5, of which waited for: 2 -> 2; matrix products, arithmetic and copies ran while one was open for 0% -> 0% of each run, Pallas kernels for 2% -> 2%
where the time goes in v6:
time: 143 us
  blocking collectives  68.8 us (48%)
  starting transfers between devices  53.6 us (37%)
  Pallas kernels  10 us (7%)
  waiting for transfers between devices  9.39 us (7%)
    all_to_all x4, blocking collectives, exchange(): lax.all_to_all(x, axis, 0, 0, axis_index_groups=[list(order)], tiled=True)  59.3 us
    ppermute x4, starting transfers between devices, reach_owners(): groups.append(lax.ppermute(total, 'wide', pairs))  31.1 us
    all_to_all x1, starting transfers between devices, exchange(): lax.all_to_all(x, axis, 0, 0, axis_index_groups=[list(order)], tiled=True)  22.5 us
    pallas_call x12, Pallas kernels, on_chip(): pl.pallas_call(kernel, out_shape=outs, in_specs=specs, out_specs=[pl.Bloc...  10 us
    all_to_all x1, blocking collectives, local(): sums = lax.all_to_all(sums, 'fsdp', 0, 0, tiled=True)  9.46 us
    all_to_all x1, waiting for transfers between devices, exchange(): lax.all_to_all(x, axis, 0, 0, axis_index_groups=[list(order)], tiled=True)  9.04 us
  transfers between devices with their start and end apart: 5, of which 2 were waited for; matrix products, arithmetic and copies ran while one was open for 0% of the time, Pallas kernels for 2%

profile of v6, /device:TPU:8, one launch (start us, length us, event | category | flops | bytes accessed | tf_op | source)
XLA Modules:
  0.0 142.6 jit_solution(14399729977080333573)
XLA Ops:
  0.6 2.2 %summary.1 = (f32[16,24,128]{2,1,0:T(8,128)S(1)}, f32[8,256]{1,0:T(8,128)S(1)}, f32[256,16]{1,0:T(8,128)S(1)}) custom-call(s32[256]{0:T(256)} %segment_ref.1, f32[4,256]{1,0:T(4,128)} %decay_ref.1, bf16[256,384]{1,0:T(8,128)(2,1)} %key_ref.7, bf16[256,384]{1,0:T(8,128)(2,1)} %value_ref.7), custom_call_target="tpu_custom_call" | custom-call | flops 50331648 | bytes 398336 | tf_op jit(solution)/shard_map/summary/pallas_call | solution.py:44
  2.9 23.9 %all_to_all.30.pieces_ref = f32[16,24,128]{2,1,0:T(8,128)S(1)} all-to-all(f32[16,24,128]{2,1,0:T(8,128)S(1)} %get-tuple-element.31), channel_id=1, replica_groups={{40,8,16,24,32,0,48,56,64,72,80,88,96,104,112,120},{41,9,17,25,33,1,49,..., dimensions={0} | all-to-all | bytes 393216 | tf_op jit(solution)/shard_map/all_to_all | solution.py:27
  26.7 0.3 group_total.2.own_ref
  27.0 18.8 %collective-permute-start.3 = (f32[24,128]{1,0:T(8,128)S(1)}, f32[24,128]{1,0:T(8,128)S(1)}, u32[]{:S(2)}, u32[]{:S(2)}) collective-permute-start(f32[24,128]{1,0:T(8,128)S(1)} %group_total.2.own_ref), channel_id=1, source_target_pairs={{0,512},{128,640},{256,768},{384,896},{1,513},{129,641},{257,769},... | collective-permute-start | bytes 36872 | tf_op jit(solution)/shard_map/ppermute | solution.py:290
  45.8 7.9 %collective-permute-start.2 = (f32[24,128]{1,0:T(8,128)S(1)}, f32[24,128]{1,0:T(8,128)S(1)}, u32[]{:S(2)}, u32[]{:S(2)}) collective-permute-start(f32[24,128]{1,0:T(8,128)S(1)} %group_total.2.own_ref), channel_id=1, source_target_pairs={{0,384},{128,512},{256,640},{384,768},{512,896},{1,385},{129,513},... | collective-permute-start | bytes 36872 | tf_op jit(solution)/shard_map/ppermute | solution.py:290
  53.8 1.3 collective-permute-start.1
  55.1 3.1 %collective-permute-start = (f32[24,128]{1,0:T(8,128)S(1)}, f32[24,128]{1,0:T(8,128)S(1)}, u32[]{:S(2)}, u32[]{:S(2)}) collective-permute-start(f32[24,128]{1,0:T(8,128)S(1)} %group_total.2.own_ref), channel_id=1, source_target_pairs={{0,128},{128,256},{256,384},{384,512},{512,640},{640,768},{768,896... | collective-permute-start | bytes 36872 | tf_op jit(solution)/shard_map/ppermute | solution.py:290
  58.2 0.5 inside.1
  58.7 0.4 local_prefix.2
  59.2 0.3 collective-permute-done.refs_0_
  59.5 0.2 group_prefix.2
  59.8 11.8 %all_to_all.31.states_ref = f32[16,24,128]{2,1,0:T(8,128)S(1)} all-to-all(f32[16,24,128]{2,1,0:T(8,128)S(1)} %group_prefix.2), channel_id=1, replica_groups={{40,8,16,24,32,0,48,56,64,72,80,88,96,104,112,120},{41,9,17,25,33,1,49,..., dimensions={0} | all-to-all | bytes 393216 | tf_op jit(solution)/shard_map/all_to_all | solution.py:27
  71.6 0.6 attention.1
  72.3 9.5 %all_to_all.32.sums_ref = f32[8,2,256]{2,1,0:T(2,128)S(1)} all-to-all(f32[8,2,256]{2,1,0:T(2,128)S(1)} %get-tuple-element.36), channel_id=1, replica_groups=mesh['wide'=8,'near'=16,'fsdp'=8] {'fsdp'}, dimensions={0} | all-to-all | bytes 32768 | tf_op jit(solution)/shard_map/all_to_all | solution.py:352
  81.7 1.0 gradient.1
  82.8 11.7 %all_to_all.33.pieces_ref = f32[16,24,128]{2,1,0:T(8,128)S(1)} all-to-all(f32[16,24,128]{2,1,0:T(8,128)S(1)} %get-tuple-element.42), channel_id=1, replica_groups={{40,8,16,24,32,0,48,56,64,72,80,88,96,104,112,120},{41,9,17,25,33,1,49,..., dimensions={0} | all-to-all | bytes 393216 | tf_op jit(solution)/shard_map/all_to_all | solution.py:27
  94.4 0.9 group_total.3
  95.3 22.5 %all-to-all-start.4 = ((f32[8,24,128]{2,1,0:T(8,128)}), f32[8,24,128]{2,1,0:T(8,128)S(1)}, u32[]{:S(2)}, u32[]{:S(2)}) async-start(f32[8,24,128]{2,1,0:T(8,128)} %group_total.3), calls=%async_computation.4 | async-start | bytes 196608 | tf_op jit(solution)/shard_map/all_to_all | solution.py:27
  117.8 1.8 %inside_back.1 = (bf16[256,384]{1,0:T(8,128)(2,1)}, f32[256,384]{1,0:T(8,128)S(1)}, f32[256,384]{1,0:T(8,128)S(1)}, bf16[256,384]{1,0:T(8,128)(2,1)}, f32[8,128]{1,0:T(8,128)S(1)}) custom-call(f32[8,256]{1,0:T(8,128)S(1)} %get-tuple-element.28.rows_ref, f32[256,16]{1,0:T(8,128)S(1)} %get-tuple-element.29.cols_ref, bf16[256,384]{1,0:T(8,128)(2,1)S(1)} %copy-done, ...), custom_call_target="tpu_custom_call" | custom-call | flops 402653184 | bytes 2328064 | tf_op jit(solution)/shard_map/inside_back/pallas_call | solution.py:44
  119.6 0.4 local_prefix.3
  120.0 9.0 %all-to-all-done.4.groups_ref = f32[8,24,128]{2,1,0:T(8,128)S(1)} async-done(((f32[8,24,128]{2,1,0:T(8,128)}), f32[8,24,128]{2,1,0:T(8,128)S(1)}, u32[]{:S(2)}, u32[]{:S(2)}) %all-to-all-start.4) | async-done | bytes 98336 | tf_op jit(solution)/shard_map/all_to_all | solution.py:27
  129.0 0.2 group_prefix.3
  129.2 11.9 %all_to_all.34.states_ref = f32[16,24,128]{2,1,0:T(8,128)S(1)} all-to-all(f32[16,24,128]{2,1,0:T(8,128)S(1)} %group_prefix.3), channel_id=1, replica_groups={{40,8,16,24,32,0,48,56,64,72,80,88,96,104,112,120},{41,9,17,25,33,1,49,..., dimensions={0} | all-to-all | bytes 393216 | tf_op jit(solution)/shard_map/all_to_all | solution.py:27
  141.2 1.4 last.1
  (13 shorter events, 0.0 us)
Async XLA Ops:
  2.8 55.3 %copy-start.1 = (bf16[256,384]{1,0:T(8,128)(2,1)S(1)}, bf16[256,384]{1,0:T(8,128)(2,1)}, u32[]{:S(2)}) copy-start(bf16[256,384]{1,0:T(8,128)(2,1)} %key_ref.7) | copy-start | bytes 589828
  2.9 55.3 %copy-start.2 = (bf16[256,384]{1,0:T(8,128)(2,1)S(1)}, bf16[256,384]{1,0:T(8,128)(2,1)}, u32[]{:S(2)}) copy-start(bf16[256,384]{1,0:T(8,128)(2,1)} %value_ref.7) | copy-start | bytes 589828
  26.7 31.4 %copy-start = (bf16[256,384]{1,0:T(8,128)(2,1)S(1)}, bf16[256,384]{1,0:T(8,128)(2,1)}, u32[]{:S(2)}) copy-start(bf16[256,384]{1,0:T(8,128)(2,1)} %query_ref.7) | copy-start | bytes 589828
  27.0 32.2 %collective-permute-start.3 = (f32[24,128]{1,0:T(8,128)S(1)}, f32[24,128]{1,0:T(8,128)S(1)}, u32[]{:S(2)}, u32[]{:S(2)}) collective-permute-start(f32[24,128]{1,0:T(8,128)S(1)} %group_total.2.own_ref), channel_id=1, source_target_pairs={{0,512},{128,640},{256,768},{384,896},{1,513},{129,641},{257,769},... | collective-permute-start | bytes 36872 | tf_op jit(solution)/shard_map/ppermute | solution.py:290
  45.8 13.4 %collective-permute-start.2 = (f32[24,128]{1,0:T(8,128)S(1)}, f32[24,128]{1,0:T(8,128)S(1)}, u32[]{:S(2)}, u32[]{:S(2)}) collective-permute-start(f32[24,128]{1,0:T(8,128)S(1)} %group_total.2.own_ref), channel_id=1, source_target_pairs={{0,384},{128,512},{256,640},{384,768},{512,896},{1,385},{129,513},... | collective-permute-start | bytes 36872 | tf_op jit(solution)/shard_map/ppermute | solution.py:290
  53.8 5.4 %collective-permute-start.1 = (f32[24,128]{1,0:T(8,128)S(1)}, f32[24,128]{1,0:T(8,128)S(1)}, u32[]{:S(2)}, u32[]{:S(2)}) collective-permute-start(f32[24,128]{1,0:T(8,128)S(1)} %group_total.2.own_ref), channel_id=1, source_target_pairs={{0,256},{128,384},{256,512},{384,640},{512,768},{640,896},{1,257},... | collective-permute-start | bytes 36872 | tf_op jit(solution)/shard_map/ppermute | solution.py:290
  55.1 4.5 %collective-permute-start = (f32[24,128]{1,0:T(8,128)S(1)}, f32[24,128]{1,0:T(8,128)S(1)}, u32[]{:S(2)}, u32[]{:S(2)}) collective-permute-start(f32[24,128]{1,0:T(8,128)S(1)} %group_total.2.own_ref), channel_id=1, source_target_pairs={{0,128},{128,256},{256,384},{384,512},{512,640},{640,768},{768,896... | collective-permute-start | bytes 36872 | tf_op jit(solution)/shard_map/ppermute | solution.py:290
  59.8 11.8 %copy-start.3 = (bf16[256,384]{1,0:T(8,128)(2,1)S(1)}, bf16[256,384]{1,0:T(8,128)(2,1)}, u32[]{:S(2)}) copy-start(bf16[256,384]{1,0:T(8,128)(2,1)} %grad_ref.3) | copy-start | bytes 589828
  59.8 11.8 %copy-start.4 = (f32[384]{0:T(512)S(1)}, f32[384]{0:T(512)}, u32[]{:S(2)}) copy-start(f32[384]{0:T(512)} %gain_ref.5) | copy-start | bytes 4612
  95.3 33.7 %all-to-all-start.4 = ((f32[8,24,128]{2,1,0:T(8,128)}), f32[8,24,128]{2,1,0:T(8,128)S(1)}, u32[]{:S(2)}, u32[]{:S(2)}) async-start(f32[8,24,128]{2,1,0:T(8,128)} %group_total.3), calls=%async_computation.4 | async-start | bytes 196608 | tf_op jit(solution)/shard_map/all_to_all | solution.py:27

commit v7 on v5

--- a/solution.py
+++ b/solution.py
@@ -17,13 +17,18 @@
 HEADS, HEAD, TILE = 4, 96, 128
 SUB = 24
 NEAR_ORDER = (5, 1, 2, 3, 4, 0, 6, 7, 8, 9, 10, 11, 12, 13, 14, 15)
-WIDE_ORDER = (4, 5, 6, 7, 0, 1, 2, 3)
+FORWARD_WIDE_ORDER = (5, 6, 7, 0, 1, 2, 3, 4)
+BACKWARD_WIDE_ORDER = (4, 5, 6, 7, 0, 1, 2, 3)
 STARTS = tuple(HEAD * h % TILE for h in range(HEADS))
 WINDOWS = tuple((HEAD * h // TILE, (HEAD * h + HEAD - 1) // TILE + 1) for h in range(HEADS))
 
 
 def exchange(x, axis, order):
     return lax.all_to_all(x, axis, 0, 0, axis_index_groups=[list(order)], tiled=True)
+
+
+def wide_order(backward):
+    return BACKWARD_WIDE_ORDER if backward else FORWARD_WIDE_ORDER
 
 
 def places(order, backward):
@@ -279,7 +284,7 @@
         [pieces],
         "group_total",
     )
-    groups = exchange(total, "wide", WIDE_ORDER)
+    groups = exchange(total, "wide", wide_order(backward))
     inside = on_chip(
         functools.partial(local_prefix_kernel, backward),
         [pltpu.VMEM(pieces.shape, jnp.float32), pltpu.VMEM(pieces.shape, jnp.float32)],
@@ -441,12 +446,12 @@
     running = jnp.zeros((rows, lanes), jnp.float32)
     gain = jnp.zeros((rows, lanes), jnp.float32)
     entering = running
-    order = places(WIDE_ORDER, backward)
+    order = places(wide_order(backward), backward)
     passes, near, far = columns(groups_ref, group_count)
     for at, g in enumerate(order):
         if at:
             running = running * (far[order[at - 1]] == near[g]).astype(jnp.float32)
-        entering = jnp.where(mine == WIDE_ORDER[g], running, entering)
+        entering = jnp.where(mine == wide_order(backward)[g], running, entering)
         piece = groups_ref[g]
         running = piece + passes[g] * running
         gain = gain + piece

time: 139 us -> 138 us (level)
  waiting for transfers between devices: 8.11 us -> 13.7 us
  starting transfers between devices: 45.9 us -> 41.3 us
  blocking collectives: 73.2 us -> 71.1 us
    all_to_all x2, waiting for transfers between devices: 8.11 us -> 13.7 us  [exchange(): lax.all_to_all(x, axis, 0, 0, axis_index_groups=[list(order)], tiled=True)]
    all_to_all x2, starting transfers between devices: 45.9 us -> 41.3 us  [exchange(): lax.all_to_all(x, axis, 0, 0, axis_index_groups=[list(order)], tiled=True)]
    all_to_all x4, blocking collectives: 63.7 us -> 61.7 us  [exchange(): lax.all_to_all(x, axis, 0, 0, axis_index_groups=[list(order)], tiled=True)]
where the time goes in v7:
time: 138 us
  blocking collectives  71.1 us (52%)
  starting transfers between devices  41.3 us (30%)
  waiting for transfers between devices  13.7 us (10%)
  Pallas kernels  10.6 us (8%)
    all_to_all x4, blocking collectives, exchange(): lax.all_to_all(x, axis, 0, 0, axis_index_groups=[list(order)], tiled=True)  61.7 us
    all_to_all x2, starting transfers between devices, exchange(): lax.all_to_all(x, axis, 0, 0, axis_index_groups=[list(order)], tiled=True)  41.3 us
    all_to_all x2, waiting for transfers between devices, exchange(): lax.all_to_all(x, axis, 0, 0, axis_index_groups=[list(order)], tiled=True)  13.7 us
    pallas_call x12, Pallas kernels, on_chip(): pl.pallas_call(kernel, out_shape=outs, in_specs=specs, out_specs=[pl.Bloc...  10.6 us
    all_to_all x1, blocking collectives, local(): sums = lax.all_to_all(sums, 'fsdp', 0, 0, tiled=True)  9.46 us
  transfers between devices with their start and end apart: 2, of which 2 were waited for; matrix products, arithmetic and copies ran while one was open for 0% of the time, Pallas kernels for 2%

profile of v7, /device:TPU:8, one launch (start us, length us, event | category | flops | bytes accessed | tf_op | source)
XLA Modules:
  0.0 137.5 jit_solution(642883460988240455)
XLA Ops:
  0.6 2.2 %summary.1 = (f32[16,24,128]{2,1,0:T(8,128)S(1)}, f32[8,256]{1,0:T(8,128)S(1)}, f32[256,16]{1,0:T(8,128)S(1)}) custom-call(s32[256]{0:T(256)} %segment_ref.1, f32[4,256]{1,0:T(4,128)} %decay_ref.1, bf16[256,384]{1,0:T(8,128)(2,1)} %key_ref.7, bf16[256,384]{1,0:T(8,128)(2,1)} %value_ref.7), custom_call_target="tpu_custom_call" | custom-call | flops 50331648 | bytes 398336 | tf_op jit(solution)/shard_map/summary/pallas_call | solution.py:48
  2.8 0.0 copy-start.2
  2.9 23.9 %all_to_all.35.pieces_ref = f32[16,24,128]{2,1,0:T(8,128)S(1)} all-to-all(f32[16,24,128]{2,1,0:T(8,128)S(1)} %get-tuple-element.31), channel_id=1, replica_groups={{40,8,16,24,32,0,48,56,64,72,80,88,96,104,112,120},{41,9,17,25,33,1,49,..., dimensions={0} | all-to-all | bytes 393216 | tf_op jit(solution)/shard_map/all_to_all | solution.py:27
  26.7 0.9 group_total.2
  27.6 19.6 %all-to-all-start.1 = ((f32[8,24,128]{2,1,0:T(8,128)}), f32[8,24,128]{2,1,0:T(8,128)S(1)}, u32[]{:S(2)}, u32[]{:S(2)}) async-start(f32[8,24,128]{2,1,0:T(8,128)} %group_total.2), calls=%async_computation.1 | async-start | bytes 196608 | tf_op jit(solution)/shard_map/all_to_all | solution.py:27
  47.3 0.6 inside.1
  47.8 0.4 local_prefix.2
  48.3 10.3 %all-to-all-done.1.groups_ref = f32[8,24,128]{2,1,0:T(8,128)S(1)} async-done(((f32[8,24,128]{2,1,0:T(8,128)}), f32[8,24,128]{2,1,0:T(8,128)S(1)}, u32[]{:S(2)}, u32[]{:S(2)}) %all-to-all-start.1) | async-done | bytes 98336 | tf_op jit(solution)/shard_map/all_to_all | solution.py:27
  58.5 0.2 group_prefix.2
  58.7 0.0 copy-start.3
  58.7 0.0 copy-start.4
  58.7 12.1 %all_to_all.36.states_ref = f32[16,24,128]{2,1,0:T(8,128)S(1)} all-to-all(f32[16,24,128]{2,1,0:T(8,128)S(1)} %group_prefix.2), channel_id=1, replica_groups={{40,8,16,24,32,0,48,56,64,72,80,88,96,104,112,120},{41,9,17,25,33,1,49,..., dimensions={0} | all-to-all | bytes 393216 | tf_op jit(solution)/shard_map/all_to_all | solution.py:27
  70.8 0.6 attention.1
  71.4 9.5 %all_to_all.37.sums_ref = f32[8,2,256]{2,1,0:T(2,128)S(1)} all-to-all(f32[8,2,256]{2,1,0:T(2,128)S(1)} %get-tuple-element.36), channel_id=1, replica_groups=mesh['wide'=8,'near'=16,'fsdp'=8] {'fsdp'}, dimensions={0} | all-to-all | bytes 32768 | tf_op jit(solution)/shard_map/all_to_all | solution.py:349
  80.9 1.0 gradient.1
  81.9 11.8 %all_to_all.38.pieces_ref = f32[16,24,128]{2,1,0:T(8,128)S(1)} all-to-all(f32[16,24,128]{2,1,0:T(8,128)S(1)} %get-tuple-element.42), channel_id=1, replica_groups={{40,8,16,24,32,0,48,56,64,72,80,88,96,104,112,120},{41,9,17,25,33,1,49,..., dimensions={0} | all-to-all | bytes 393216 | tf_op jit(solution)/shard_map/all_to_all | solution.py:27
  93.7 0.9 group_total.3
  94.6 21.7 %all-to-all-start.5 = ((f32[8,24,128]{2,1,0:T(8,128)}), f32[8,24,128]{2,1,0:T(8,128)S(1)}, u32[]{:S(2)}, u32[]{:S(2)}) async-start(f32[8,24,128]{2,1,0:T(8,128)} %group_total.3), calls=%async_computation.5 | async-start | bytes 196608 | tf_op jit(solution)/shard_map/all_to_all | solution.py:27
  116.4 1.8 %inside_back.1 = (bf16[256,384]{1,0:T(8,128)(2,1)}, f32[256,384]{1,0:T(8,128)S(1)}, f32[256,384]{1,0:T(8,128)S(1)}, bf16[256,384]{1,0:T(8,128)(2,1)}, f32[8,128]{1,0:T(8,128)S(1)}) custom-call(f32[8,256]{1,0:T(8,128)S(1)} %get-tuple-element.28.rows_ref, f32[256,16]{1,0:T(8,128)S(1)} %get-tuple-element.29.cols_ref, bf16[256,384]{1,0:T(8,128)(2,1)S(1)} %copy-done, ...), custom_call_target="tpu_custom_call" | custom-call | flops 402653184 | bytes 2328064 | tf_op jit(solution)/shard_map/inside_back/pallas_call | solution.py:48
  118.1 0.4 local_prefix.3
  118.6 3.4 %all-to-all-done.5.groups_ref = f32[8,24,128]{2,1,0:T(8,128)S(1)} async-done(((f32[8,24,128]{2,1,0:T(8,128)}), f32[8,24,128]{2,1,0:T(8,128)S(1)}, u32[]{:S(2)}, u32[]{:S(2)}) %all-to-all-start.5) | async-done | bytes 98336 | tf_op jit(solution)/shard_map/all_to_all | solution.py:27
  122.0 0.2 group_prefix.3
  122.2 13.9 %all_to_all.39.states_ref = f32[16,24,128]{2,1,0:T(8,128)S(1)} all-to-all(f32[16,24,128]{2,1,0:T(8,128)S(1)} %group_prefix.3), channel_id=1, replica_groups={{40,8,16,24,32,0,48,56,64,72,80,88,96,104,112,120},{41,9,17,25,33,1,49,..., dimensions={0} | all-to-all | bytes 393216 | tf_op jit(solution)/shard_map/all_to_all | solution.py:27
  136.1 1.4 %last.1 = (bf16[256,384]{1,0:T(8,128)(2,1)}, bf16[256,384]{1,0:T(8,128)(2,1)}, f32[384]{0:T(512)}) custom-call(f32[16,24,128]{2,1,0:T(8,128)S(1)} %all_to_all.39.states_ref, f32[256,16]{1,0:T(8,128)S(1)} %get-tuple-element.29.cols_ref, bf16[256,384]{1,0:T(8,128)(2,1)S(1)} %copy-done.1, bf16[256,384]{1,0:T(8,128)(2,1)S(1)} %copy-done.2, ...), custom_call_target="tpu_custom_call" | custom-call | flops 201326592 | bytes 1787392 | tf_op jit(solution)/shard_map/last/pallas_call | solution.py:48
  (7 shorter events, 0.0 us)
Async XLA Ops:
  2.8 44.4 %copy-start.2 = (bf16[256,384]{1,0:T(8,128)(2,1)S(1)}, bf16[256,384]{1,0:T(8,128)(2,1)}, u32[]{:S(2)}) copy-start(bf16[256,384]{1,0:T(8,128)(2,1)} %value_ref.7) | copy-start | bytes 589828
  26.7 20.5 %copy-start = (bf16[256,384]{1,0:T(8,128)(2,1)S(1)}, bf16[256,384]{1,0:T(8,128)(2,1)}, u32[]{:S(2)}) copy-start(bf16[256,384]{1,0:T(8,128)(2,1)} %query_ref.7) | copy-start | bytes 589828
  26.7 20.5 %copy-start.1 = (bf16[256,384]{1,0:T(8,128)(2,1)S(1)}, bf16[256,384]{1,0:T(8,128)(2,1)}, u32[]{:S(2)}) copy-start(bf16[256,384]{1,0:T(8,128)(2,1)} %key_ref.7) | copy-start | bytes 589828
  27.6 30.9 %all-to-all-start.1 = ((f32[8,24,128]{2,1,0:T(8,128)}), f32[8,24,128]{2,1,0:T(8,128)S(1)}, u32[]{:S(2)}, u32[]{:S(2)}) async-start(f32[8,24,128]{2,1,0:T(8,128)} %group_total.2), calls=%async_computation.1 | async-start | bytes 196608 | tf_op jit(solution)/shard_map/all_to_all | solution.py:27
  58.7 12.1 %copy-start.3 = (bf16[256,384]{1,0:T(8,128)(2,1)S(1)}, bf16[256,384]{1,0:T(8,128)(2,1)}, u32[]{:S(2)}) copy-start(bf16[256,384]{1,0:T(8,128)(2,1)} %grad_ref.3) | copy-start | bytes 589828
  58.7 12.1 %copy-start.4 = (f32[384]{0:T(512)S(1)}, f32[384]{0:T(512)}, u32[]{:S(2)}) copy-start(f32[384]{0:T(512)} %gain_ref.5) | copy-start | bytes 4612
  94.6 27.4 %all-to-all-start.5 = ((f32[8,24,128]{2,1,0:T(8,128)}), f32[8,24,128]{2,1,0:T(8,128)S(1)}, u32[]{:S(2)}, u32[]{:S(2)}) async-start(f32[8,24,128]{2,1,0:T(8,128)} %group_total.3), calls=%async_computation.5 | async-start | bytes 196608 | tf_op jit(solution)/shard_map/all_to_all | solution.py:27

commit v8 on v7

--- a/solution.py
+++ b/solution.py
@@ -16,7 +16,7 @@
 
 HEADS, HEAD, TILE = 4, 96, 128
 SUB = 24
-NEAR_ORDER = (5, 1, 2, 3, 4, 0, 6, 7, 8, 9, 10, 11, 12, 13, 14, 15)
+NEAR_ORDER = (5, 6, 7, 8, 9, 10, 11, 12, 13, 14, 15, 0, 1, 2, 3, 4)
 FORWARD_WIDE_ORDER = (5, 6, 7, 0, 1, 2, 3, 4)
 BACKWARD_WIDE_ORDER = (4, 5, 6, 7, 0, 1, 2, 3)
 STARTS = tuple(HEAD * h % TILE for h in range(HEADS))

time: 138 us -> 138 us (level)
  no operation moved by 1% of the time
where the time goes in v8:
time: 138 us
  blocking collectives  71.9 us (52%)
  starting transfers between devices  41.2 us (30%)
  waiting for transfers between devices  13.3 us (10%)
  Pallas kernels  10.6 us (8%)
    all_to_all x4, blocking collectives, exchange(): lax.all_to_all(x, axis, 0, 0, axis_index_groups=[list(order)], tiled=True)  62.4 us
    all_to_all x2, starting transfers between devices, exchange(): lax.all_to_all(x, axis, 0, 0, axis_index_groups=[list(order)], tiled=True)  41.2 us
    all_to_all x2, waiting for transfers between devices, exchange(): lax.all_to_all(x, axis, 0, 0, axis_index_groups=[list(order)], tiled=True)  13.3 us
    pallas_call x12, Pallas kernels, on_chip(): pl.pallas_call(kernel, out_shape=outs, in_specs=specs, out_specs=[pl.Bloc...  10.6 us
    all_to_all x1, blocking collectives, local(): sums = lax.all_to_all(sums, 'fsdp', 0, 0, tiled=True)  9.46 us
  transfers between devices with their start and end apart: 2, of which 2 were waited for; matrix products, arithmetic and copies ran while one was open for 0% of the time, Pallas kernels for 2%

profile of v8, /device:TPU:8, one launch (start us, length us, event | category | flops | bytes accessed | tf_op | source)
XLA Modules:
  0.0 137.8 jit_solution(10460271654042078333)
XLA Ops:
  0.6 2.2 %summary.1 = (f32[16,24,128]{2,1,0:T(8,128)S(1)}, f32[8,256]{1,0:T(8,128)S(1)}, f32[256,16]{1,0:T(8,128)S(1)}) custom-call(s32[256]{0:T(256)} %segment_ref.1, f32[4,256]{1,0:T(4,128)} %decay_ref.1, bf16[256,384]{1,0:T(8,128)(2,1)} %key_ref.7, bf16[256,384]{1,0:T(8,128)(2,1)} %value_ref.7), custom_call_target="tpu_custom_call" | custom-call | flops 50331648 | bytes 398336 | tf_op jit(solution)/shard_map/summary/pallas_call | solution.py:48
  2.8 0.0 copy-start.2
  2.9 23.9 %all_to_all.35.pieces_ref = f32[16,24,128]{2,1,0:T(8,128)S(1)} all-to-all(f32[16,24,128]{2,1,0:T(8,128)S(1)} %get-tuple-element.31), channel_id=1, replica_groups={{40,48,56,64,72,80,88,96,104,112,120,0,8,16,24,32},{41,49,57,65,73,81,8..., dimensions={0} | all-to-all | bytes 393216 | tf_op jit(solution)/shard_map/all_to_all | solution.py:27
  26.7 0.9 group_total.2
  27.6 19.6 %all-to-all-start.1 = ((f32[8,24,128]{2,1,0:T(8,128)}), f32[8,24,128]{2,1,0:T(8,128)S(1)}, u32[]{:S(2)}, u32[]{:S(2)}) async-start(f32[8,24,128]{2,1,0:T(8,128)} %group_total.2), calls=%async_computation.1 | async-start | bytes 196608 | tf_op jit(solution)/shard_map/all_to_all | solution.py:27
  47.3 0.5 inside.1
  47.8 0.4 local_prefix.2
  48.2 10.2 %all-to-all-done.1.groups_ref = f32[8,24,128]{2,1,0:T(8,128)S(1)} async-done(((f32[8,24,128]{2,1,0:T(8,128)}), f32[8,24,128]{2,1,0:T(8,128)S(1)}, u32[]{:S(2)}, u32[]{:S(2)}) %all-to-all-start.1) | async-done | bytes 98336 | tf_op jit(solution)/shard_map/all_to_all | solution.py:27
  58.5 0.2 group_prefix.2
  58.7 0.0 copy-start.3
  58.7 0.0 copy-start.4
  58.7 12.5 %all_to_all.36.states_ref = f32[16,24,128]{2,1,0:T(8,128)S(1)} all-to-all(f32[16,24,128]{2,1,0:T(8,128)S(1)} %group_prefix.2), channel_id=1, replica_groups={{40,48,56,64,72,80,88,96,104,112,120,0,8,16,24,32},{41,49,57,65,73,81,8..., dimensions={0} | all-to-all | bytes 393216 | tf_op jit(solution)/shard_map/all_to_all | solution.py:27
  71.2 0.6 attention.1
  71.8 9.5 %all_to_all.37.sums_ref = f32[8,2,256]{2,1,0:T(2,128)S(1)} all-to-all(f32[8,2,256]{2,1,0:T(2,128)S(1)} %get-tuple-element.36), channel_id=1, replica_groups=mesh['wide'=8,'near'=16,'fsdp'=8] {'fsdp'}, dimensions={0} | all-to-all | bytes 32768 | tf_op jit(solution)/shard_map/all_to_all | solution.py:349
  81.3 1.0 gradient.1
  82.3 11.8 %all_to_all.38.pieces_ref = f32[16,24,128]{2,1,0:T(8,128)S(1)} all-to-all(f32[16,24,128]{2,1,0:T(8,128)S(1)} %get-tuple-element.42), channel_id=1, replica_groups={{40,48,56,64,72,80,88,96,104,112,120,0,8,16,24,32},{41,49,57,65,73,81,8..., dimensions={0} | all-to-all | bytes 393216 | tf_op jit(solution)/shard_map/all_to_all | solution.py:27
  94.1 0.9 group_total.3
  95.0 21.6 %all-to-all-start.5 = ((f32[8,24,128]{2,1,0:T(8,128)}), f32[8,24,128]{2,1,0:T(8,128)S(1)}, u32[]{:S(2)}, u32[]{:S(2)}) async-start(f32[8,24,128]{2,1,0:T(8,128)} %group_total.3), calls=%async_computation.5 | async-start | bytes 196608 | tf_op jit(solution)/shard_map/all_to_all | solution.py:27
  116.6 1.8 %inside_back.1 = (bf16[256,384]{1,0:T(8,128)(2,1)}, f32[256,384]{1,0:T(8,128)S(1)}, f32[256,384]{1,0:T(8,128)S(1)}, bf16[256,384]{1,0:T(8,128)(2,1)}, f32[8,128]{1,0:T(8,128)S(1)}) custom-call(f32[8,256]{1,0:T(8,128)S(1)} %get-tuple-element.28.rows_ref, f32[256,16]{1,0:T(8,128)S(1)} %get-tuple-element.29.cols_ref, bf16[256,384]{1,0:T(8,128)(2,1)S(1)} %copy-done, ...), custom_call_target="tpu_custom_call" | custom-call | flops 402653184 | bytes 2328064 | tf_op jit(solution)/shard_map/inside_back/pallas_call | solution.py:48
  118.4 0.4 local_prefix.3
  118.8 3.1 %all-to-all-done.5.groups_ref = f32[8,24,128]{2,1,0:T(8,128)S(1)} async-done(((f32[8,24,128]{2,1,0:T(8,128)}), f32[8,24,128]{2,1,0:T(8,128)S(1)}, u32[]{:S(2)}, u32[]{:S(2)}) %all-to-all-start.5) | async-done | bytes 98336 | tf_op jit(solution)/shard_map/all_to_all | solution.py:27
  122.0 0.2 group_prefix.3
  122.2 14.2 %all_to_all.39.states_ref = f32[16,24,128]{2,1,0:T(8,128)S(1)} all-to-all(f32[16,24,128]{2,1,0:T(8,128)S(1)} %group_prefix.3), channel_id=1, replica_groups={{40,48,56,64,72,80,88,96,104,112,120,0,8,16,24,32},{41,49,57,65,73,81,8..., dimensions={0} | all-to-all | bytes 393216 | tf_op jit(solution)/shard_map/all_to_all | solution.py:27
  136.4 1.4 %last.1 = (bf16[256,384]{1,0:T(8,128)(2,1)}, bf16[256,384]{1,0:T(8,128)(2,1)}, f32[384]{0:T(512)}) custom-call(f32[16,24,128]{2,1,0:T(8,128)S(1)} %all_to_all.39.states_ref, f32[256,16]{1,0:T(8,128)S(1)} %get-tuple-element.29.cols_ref, bf16[256,384]{1,0:T(8,128)(2,1)S(1)} %copy-done.1, bf16[256,384]{1,0:T(8,128)(2,1)S(1)} %copy-done.2, ...), custom_call_target="tpu_custom_call" | custom-call | flops 201326592 | bytes 1787392 | tf_op jit(solution)/shard_map/last/pallas_call | solution.py:48
  (7 shorter events, 0.0 us)
Async XLA Ops:
  2.8 44.4 %copy-start.2 = (bf16[256,384]{1,0:T(8,128)(2,1)S(1)}, bf16[256,384]{1,0:T(8,128)(2,1)}, u32[]{:S(2)}) copy-start(bf16[256,384]{1,0:T(8,128)(2,1)} %value_ref.7) | copy-start | bytes 589828
  26.7 20.5 %copy-start = (bf16[256,384]{1,0:T(8,128)(2,1)S(1)}, bf16[256,384]{1,0:T(8,128)(2,1)}, u32[]{:S(2)}) copy-start(bf16[256,384]{1,0:T(8,128)(2,1)} %query_ref.7) | copy-start | bytes 589828
  26.7 20.5 %copy-start.1 = (bf16[256,384]{1,0:T(8,128)(2,1)S(1)}, bf16[256,384]{1,0:T(8,128)(2,1)}, u32[]{:S(2)}) copy-start(bf16[256,384]{1,0:T(8,128)(2,1)} %key_ref.7) | copy-start | bytes 589828
  27.6 30.8 %all-to-all-start.1 = ((f32[8,24,128]{2,1,0:T(8,128)}), f32[8,24,128]{2,1,0:T(8,128)S(1)}, u32[]{:S(2)}, u32[]{:S(2)}) async-start(f32[8,24,128]{2,1,0:T(8,128)} %group_total.2), calls=%async_computation.1 | async-start | bytes 196608 | tf_op jit(solution)/shard_map/all_to_all | solution.py:27
  58.7 12.5 %copy-start.3 = (bf16[256,384]{1,0:T(8,128)(2,1)S(1)}, bf16[256,384]{1,0:T(8,128)(2,1)}, u32[]{:S(2)}) copy-start(bf16[256,384]{1,0:T(8,128)(2,1)} %grad_ref.3) | copy-start | bytes 589828
  58.7 12.5 %copy-start.4 = (f32[384]{0:T(512)S(1)}, f32[384]{0:T(512)}, u32[]{:S(2)}) copy-start(f32[384]{0:T(512)} %gain_ref.5) | copy-start | bytes 4612
  95.0 26.9 %all-to-all-start.5 = ((f32[8,24,128]{2,1,0:T(8,128)}), f32[8,24,128]{2,1,0:T(8,128)S(1)}, u32[]{:S(2)}, u32[]{:S(2)}) async-start(f32[8,24,128]{2,1,0:T(8,128)} %group_total.3), calls=%async_computation.5 | async-start | bytes 196608 | tf_op jit(solution)/shard_map/all_to_all | solution.py:27

commit v9 on v8

--- a/solution.py
+++ b/solution.py
@@ -17,8 +17,8 @@
 HEADS, HEAD, TILE = 4, 96, 128
 SUB = 24
 NEAR_ORDER = (5, 6, 7, 8, 9, 10, 11, 12, 13, 14, 15, 0, 1, 2, 3, 4)
-FORWARD_WIDE_ORDER = (5, 6, 7, 0, 1, 2, 3, 4)
-BACKWARD_WIDE_ORDER = (4, 5, 6, 7, 0, 1, 2, 3)
+FORWARD_WIDE_ORDER = (5, 1, 6, 2, 7, 3, 0, 4)
+BACKWARD_WIDE_ORDER = (4, 0, 5, 1, 6, 2, 7, 3)
 STARTS = tuple(HEAD * h % TILE for h in range(HEADS))
 WINDOWS = tuple((HEAD * h // TILE, (HEAD * h + HEAD - 1) // TILE + 1) for h in range(HEADS))
 

time: 138 us -> 138 us (level)
  no operation moved by 1% of the time
where the time goes in v9:
time: 138 us; the launch traced here: 137 us
  blocking collectives  71.4 us (52%)
  starting transfers between devices  41.4 us (30%)
  waiting for transfers between devices  13.1 us (9%)
  Pallas kernels  10.6 us (8%)
    all_to_all x4, blocking collectives, exchange(): lax.all_to_all(x, axis, 0, 0, axis_index_groups=[list(order)], tiled=True)  61.9 us
    all_to_all x2, starting transfers between devices, exchange(): lax.all_to_all(x, axis, 0, 0, axis_index_groups=[list(order)], tiled=True)  41.4 us
    all_to_all x2, waiting for transfers between devices, exchange(): lax.all_to_all(x, axis, 0, 0, axis_index_groups=[list(order)], tiled=True)  13.1 us
    pallas_call x12, Pallas kernels, on_chip(): pl.pallas_call(kernel, out_shape=outs, in_specs=specs, out_specs=[pl.Bloc...  10.6 us
    all_to_all x1, blocking collectives, local(): sums = lax.all_to_all(sums, 'fsdp', 0, 0, tiled=True)  9.45 us
  transfers between devices with their start and end apart: 2, of which 2 were waited for; matrix products, arithmetic and copies ran while one was open for 0% of the time, Pallas kernels for 2%

profile of v9, /device:TPU:8, one launch (start us, length us, event | category | flops | bytes accessed | tf_op | source)
XLA Modules:
  0.0 137.3 jit_solution(7998754609967892856)
XLA Ops:
  0.6 2.2 %summary.1 = (f32[16,24,128]{2,1,0:T(8,128)S(1)}, f32[8,256]{1,0:T(8,128)S(1)}, f32[256,16]{1,0:T(8,128)S(1)}) custom-call(s32[256]{0:T(256)} %segment_ref.1, f32[4,256]{1,0:T(4,128)} %decay_ref.1, bf16[256,384]{1,0:T(8,128)(2,1)} %key_ref.7, bf16[256,384]{1,0:T(8,128)(2,1)} %value_ref.7), custom_call_target="tpu_custom_call" | custom-call | flops 50331648 | bytes 398336 | tf_op jit(solution)/shard_map/summary/pallas_call | solution.py:48
  2.8 0.0 copy-start.2
  2.9 23.9 %all_to_all.35.pieces_ref = f32[16,24,128]{2,1,0:T(8,128)S(1)} all-to-all(f32[16,24,128]{2,1,0:T(8,128)S(1)} %get-tuple-element.31), channel_id=1, replica_groups={{40,48,56,64,72,80,88,96,104,112,120,0,8,16,24,32},{41,49,57,65,73,81,8..., dimensions={0} | all-to-all | bytes 393216 | tf_op jit(solution)/shard_map/all_to_all | solution.py:27
  26.7 0.9 group_total.2
  27.6 19.6 %all-to-all-start.1 = ((f32[8,24,128]{2,1,0:T(8,128)}), f32[8,24,128]{2,1,0:T(8,128)S(1)}, u32[]{:S(2)}, u32[]{:S(2)}) async-start(f32[8,24,128]{2,1,0:T(8,128)} %group_total.2), calls=%async_computation.1 | async-start | bytes 196608 | tf_op jit(solution)/shard_map/all_to_all | solution.py:27
  47.3 0.6 inside.1
  47.8 0.4 local_prefix.2
  48.3 9.0 %all-to-all-done.1.groups_ref = f32[8,24,128]{2,1,0:T(8,128)S(1)} async-done(((f32[8,24,128]{2,1,0:T(8,128)}), f32[8,24,128]{2,1,0:T(8,128)S(1)}, u32[]{:S(2)}, u32[]{:S(2)}) %all-to-all-start.1) | async-done | bytes 98336 | tf_op jit(solution)/shard_map/all_to_all | solution.py:27
  57.3 0.2 group_prefix.2
  57.5 0.0 copy-start.3
  57.5 0.0 copy-start.4
  57.5 13.4 %all_to_all.36.states_ref = f32[16,24,128]{2,1,0:T(8,128)S(1)} all-to-all(f32[16,24,128]{2,1,0:T(8,128)S(1)} %group_prefix.2), channel_id=1, replica_groups={{40,48,56,64,72,80,88,96,104,112,120,0,8,16,24,32},{41,49,57,65,73,81,8..., dimensions={0} | all-to-all | bytes 393216 | tf_op jit(solution)/shard_map/all_to_all | solution.py:27
  70.9 0.6 attention.1
  71.6 9.5 %all_to_all.37.sums_ref = f32[8,2,256]{2,1,0:T(2,128)S(1)} all-to-all(f32[8,2,256]{2,1,0:T(2,128)S(1)} %get-tuple-element.36), channel_id=1, replica_groups=mesh['wide'=8,'near'=16,'fsdp'=8] {'fsdp'}, dimensions={0} | all-to-all | bytes 32768 | tf_op jit(solution)/shard_map/all_to_all | solution.py:349
  81.0 1.0 gradient.1
  82.0 11.7 %all_to_all.38.pieces_ref = f32[16,24,128]{2,1,0:T(8,128)S(1)} all-to-all(f32[16,24,128]{2,1,0:T(8,128)S(1)} %get-tuple-element.42), channel_id=1, replica_groups={{40,48,56,64,72,80,88,96,104,112,120,0,8,16,24,32},{41,49,57,65,73,81,8..., dimensions={0} | all-to-all | bytes 393216 | tf_op jit(solution)/shard_map/all_to_all | solution.py:27
  93.7 0.9 group_total.3
  94.6 21.7 %all-to-all-start.5 = ((f32[8,24,128]{2,1,0:T(8,128)}), f32[8,24,128]{2,1,0:T(8,128)S(1)}, u32[]{:S(2)}, u32[]{:S(2)}) async-start(f32[8,24,128]{2,1,0:T(8,128)} %group_total.3), calls=%async_computation.5 | async-start | bytes 196608 | tf_op jit(solution)/shard_map/all_to_all | solution.py:27
  116.4 1.8 %inside_back.1 = (bf16[256,384]{1,0:T(8,128)(2,1)}, f32[256,384]{1,0:T(8,128)S(1)}, f32[256,384]{1,0:T(8,128)S(1)}, bf16[256,384]{1,0:T(8,128)(2,1)}, f32[8,128]{1,0:T(8,128)S(1)}) custom-call(f32[8,256]{1,0:T(8,128)S(1)} %get-tuple-element.28.rows_ref, f32[256,16]{1,0:T(8,128)S(1)} %get-tuple-element.29.cols_ref, bf16[256,384]{1,0:T(8,128)(2,1)S(1)} %copy-done, ...), custom_call_target="tpu_custom_call" | custom-call | flops 402653184 | bytes 2328064 | tf_op jit(solution)/shard_map/inside_back/pallas_call | solution.py:48
  118.1 0.4 local_prefix.3
  118.6 4.1 %all-to-all-done.5.groups_ref = f32[8,24,128]{2,1,0:T(8,128)S(1)} async-done(((f32[8,24,128]{2,1,0:T(8,128)}), f32[8,24,128]{2,1,0:T(8,128)S(1)}, u32[]{:S(2)}, u32[]{:S(2)}) %all-to-all-start.5) | async-done | bytes 98336 | tf_op jit(solution)/shard_map/all_to_all | solution.py:27
  122.6 0.2 group_prefix.3
  122.8 13.0 %all_to_all.39.states_ref = f32[16,24,128]{2,1,0:T(8,128)S(1)} all-to-all(f32[16,24,128]{2,1,0:T(8,128)S(1)} %group_prefix.3), channel_id=1, replica_groups={{40,48,56,64,72,80,88,96,104,112,120,0,8,16,24,32},{41,49,57,65,73,81,8..., dimensions={0} | all-to-all | bytes 393216 | tf_op jit(solution)/shard_map/all_to_all | solution.py:27
  135.8 1.4 %last.1 = (bf16[256,384]{1,0:T(8,128)(2,1)}, bf16[256,384]{1,0:T(8,128)(2,1)}, f32[384]{0:T(512)}) custom-call(f32[16,24,128]{2,1,0:T(8,128)S(1)} %all_to_all.39.states_ref, f32[256,16]{1,0:T(8,128)S(1)} %get-tuple-element.29.cols_ref, bf16[256,384]{1,0:T(8,128)(2,1)S(1)} %copy-done.1, bf16[256,384]{1,0:T(8,128)(2,1)S(1)} %copy-done.2, ...), custom_call_target="tpu_custom_call" | custom-call | flops 201326592 | bytes 1787392 | tf_op jit(solution)/shard_map/last/pallas_call | solution.py:48
  (7 shorter events, 0.0 us)
Async XLA Ops:
  2.8 44.4 %copy-start.2 = (bf16[256,384]{1,0:T(8,128)(2,1)S(1)}, bf16[256,384]{1,0:T(8,128)(2,1)}, u32[]{:S(2)}) copy-start(bf16[256,384]{1,0:T(8,128)(2,1)} %value_ref.7) | copy-start | bytes 589828
  26.7 20.5 %copy-start = (bf16[256,384]{1,0:T(8,128)(2,1)S(1)}, bf16[256,384]{1,0:T(8,128)(2,1)}, u32[]{:S(2)}) copy-start(bf16[256,384]{1,0:T(8,128)(2,1)} %query_ref.7) | copy-start | bytes 589828
  26.7 20.5 %copy-start.1 = (bf16[256,384]{1,0:T(8,128)(2,1)S(1)}, bf16[256,384]{1,0:T(8,128)(2,1)}, u32[]{:S(2)}) copy-start(bf16[256,384]{1,0:T(8,128)(2,1)} %key_ref.7) | copy-start | bytes 589828
  27.6 29.6 %all-to-all-start.1 = ((f32[8,24,128]{2,1,0:T(8,128)}), f32[8,24,128]{2,1,0:T(8,128)S(1)}, u32[]{:S(2)}, u32[]{:S(2)}) async-start(f32[8,24,128]{2,1,0:T(8,128)} %group_total.2), calls=%async_computation.1 | async-start | bytes 196608 | tf_op jit(solution)/shard_map/all_to_all | solution.py:27
  57.5 13.4 %copy-start.3 = (bf16[256,384]{1,0:T(8,128)(2,1)S(1)}, bf16[256,384]{1,0:T(8,128)(2,1)}, u32[]{:S(2)}) copy-start(bf16[256,384]{1,0:T(8,128)(2,1)} %grad_ref.3) | copy-start | bytes 589828
  57.5 13.4 %copy-start.4 = (f32[384]{0:T(512)S(1)}, f32[384]{0:T(512)}, u32[]{:S(2)}) copy-start(f32[384]{0:T(512)} %gain_ref.5) | copy-start | bytes 4612
  94.6 28.0 %all-to-all-start.5 = ((f32[8,24,128]{2,1,0:T(8,128)}), f32[8,24,128]{2,1,0:T(8,128)S(1)}, u32[]{:S(2)}, u32[]{:S(2)}) async-start(f32[8,24,128]{2,1,0:T(8,128)} %group_total.3), calls=%async_computation.5 | async-start | bytes 196608 | tf_op jit(solution)/shard_map/all_to_all | solution.py:27
